TPU v7x, 128 devices: a whole 4x4x4 slice. The times are simulated.
128 devices in a mesh: grp: 4 (over x), ep: 32 (over z, y, core).
Axes of the slice: x: 4, y: 4, z: 4, core: 2. Of those that a mesh axis runs over, the one named last changes fastest.
Arguments:
- base_tiles: bfloat16 [128, 3584, 1024], P(('grp', 'ep')), may hold values from -1.5 to 1.5
- adjusted_tiles: bfloat16 [256, 3584, 1024], P(('grp', 'ep')), may hold values from -1.5 to 1.5
- sketch: bfloat16 [1024, 128], replicated, may hold values from -6 to 6
- base_place: int32 [128], replicated, may hold values from 0 to 127, each once
- adjusted_place: int32 [128], replicated, may hold values from 0 to 255, as said below
- owner_map: int32 [128], replicated, may hold values from 0 to 127, each once
Outputs:
- scaled_basis: float32 [128, 3584, 128], P(('grp', 'ep'))
- projected: float32 [128, 128, 1024], P(('grp', 'ep'))
Inputs may be any that keep to these rules, and one draw needn't show every extreme that they name: `base_place`: each slot once. `adjusted_place`: distinct slots; slot 2 d + s is slot s of device d; a quarter of the devices hold two adjusted windows, half hold one, a quarter none. `owner_map`: each device owns exactly one expert.
All inputs are finite; a program needn't handle non-finite values.
Results may differ from a plain program's by a relative error of at most 0.006.
Values may be sent and summed in bfloat16 or wider, within the bound.
A program may use at most 192 MiB of HBM per device.

v0:
```python
import math

import jax
import jax.numpy as jnp
from jax import lax
from jax.sharding import PartitionSpec as P

POWER = 2


highest = lax.Precision.HIGHEST


def orthonormal(columns):
    gram_matrix = lax.dot_general(
        columns,
        columns,
        (((0,), (0,)), ((), ())),
        precision=highest,
        preferred_element_type=jnp.float32,
    )
    factor_low = jnp.linalg.cholesky(gram_matrix)
    return jax.scipy.linalg.solve_triangular(factor_low, columns.T, lower=True).T


def factorize(difference, sketch):
    current = orthonormal(jnp.dot(difference, sketch, preferred_element_type=jnp.float32))
    for repeat in range(POWER):
        rounded = current.astype(jnp.bfloat16)
        across = orthonormal(
            lax.dot_general(
                difference, rounded, (((0,), (0,)), ((), ())), preferred_element_type=jnp.float32
            )
        )
        current = orthonormal(
            jnp.dot(difference, across.astype(jnp.bfloat16), preferred_element_type=jnp.float32)
        )
    rounded = current.astype(jnp.bfloat16)
    projected = lax.dot_general(
        rounded, difference, (((0,), (0,)), ((), ())), preferred_element_type=jnp.float32
    )
    return (current * math.sqrt(difference.shape[0]), projected)


def shards(base_tiles, adjusted_tiles, sketch, base_place, adjusted_place, owner_map):
    groups = lax.axis_size("grp")
    members = lax.axis_size("ep")
    count = groups * members
    rows = base_tiles.shape[1]
    width = base_tiles.shape[2]
    piece = rows // count
    base_got, adjusted_got = (
        lax.all_to_all(
            base_tiles.reshape(1, count, piece, width),
            ("grp", "ep"),
            split_axis=1,
            concat_axis=1,
            tiled=True,
        ),
        lax.all_to_all(
            adjusted_tiles.reshape(2, count, piece, width),
            ("grp", "ep"),
            split_axis=1,
            concat_axis=1,
            tiled=True,
        ),
    )
    base_flat = base_got.reshape(count, piece, width)
    adjusted_flat = adjusted_got.reshape(2 * count, piece, width)
    experts = jnp.arange(count, dtype=jnp.int32)
    holder = jnp.zeros((count,), jnp.int32).at[owner_map].set(experts)
    base_rows = jnp.take(base_flat, base_place[holder], axis=0)
    adjusted_slot = adjusted_place[holder]
    adjusted_rows = jnp.take(adjusted_flat, adjusted_slot % 2 * count + adjusted_slot // 2, axis=0)
    base_back, adjusted_back = (
        lax.all_to_all(base_rows, ("grp", "ep"), split_axis=0, concat_axis=0, tiled=True),
        lax.all_to_all(adjusted_rows, ("grp", "ep"), split_axis=0, concat_axis=0, tiled=True),
    )
    difference = (
        adjusted_back.reshape(rows, width).astype(jnp.float32)
        - base_back.reshape(rows, width).astype(jnp.float32)
    ).astype(jnp.bfloat16)
    scaled_basis, projected = factorize(difference, sketch)
    return (scaled_basis[None], projected[None])


def solution(mesh):
    in_specs = (P(("grp", "ep"), None, None), P(("grp", "ep"), None, None), P(), P(), P(), P())
    out_specs = (P(("grp", "ep"), None, None), P(("grp", "ep"), None, None))
    return jax.shard_map(shards, mesh=mesh, in_specs=in_specs, out_specs=out_specs, check_vma=False)
```

profile of v0, /device:TPU:1, one launch (start us, length us, event | category | flops | bytes accessed | tf_op | source)
XLA Modules:
  0.0 749.8 jit_solution(16035665615131525293)
XLA Ops:
  0.6 0.0 copy-start
  0.6 10.9 %reshape.141 = bf16[1,128,28,1024]{3,2,1,0:T(8,128)(2,1)} reshape(bf16[1,3584,1024]{2,1,0:T(8,128)(2,1)} %param.11) | data formatting | bytes 14680064 | tf_op jit(solution)/shard_map/reshape | solution.py:54
  11.6 12.0 %all-to-all-start.2 = ((bf16[1,128,28,1024]{3,2,0,1:T(8,128)(2,1)}), bf16[1,128,28,1024]{3,2,0,1:T(8,128)(2,1)}, u32[]{:S(2)}, u32[]{:S(2)}) async-start(bf16[1,128,28,1024]{3,2,0,1:T(8,128)(2,1)} %bitcast.115), calls=%async_computation.2 | async-start | bytes 16777216 | tf_op jit(solution)/shard_map/all_to_all | solution.py:53
  23.6 27.3 %copy.39 = bf16[2,3584,1024]{2,0,1:T(2,128)(2,1)} copy(bf16[2,3584,1024]{2,1,0:T(8,128)(2,1)} %param.12) | data formatting | bytes 29360128 | tf_op args[1]
  50.9 79.1 %all-to-all-done.2 = bf16[1,128,28,1024]{3,2,0,1:T(8,128)(2,1)} async-done(((bf16[1,128,28,1024]{3,2,0,1:T(8,128)(2,1)}), bf16[1,128,28,1024]{3,2,0,1:T(8,128)(2,1)}, u32[]{:S(2)}, u32[]{:S(2)}) %all-to-all-start.2) | async-done | bytes 7340064 | tf_op jit(solution)/shard_map/all_to_all | solution.py:53
  130.0 8.2 %all-to-all-start = ((bf16[2,128,28,1024]{3,0,2,1:T(2,128)(2,1)}), bf16[2,128,28,1024]{3,0,2,1:T(2,128)(2,1)}, u32[]{:S(2)}, u32[]{:S(2)}) async-start(bf16[2,128,28,1024]{3,0,2,1:T(2,128)(2,1)} %bitcast.113), calls=%async_computation | async-start | bytes 29360128 | tf_op jit(solution)/shard_map/all_to_all | solution.py:60
  138.3 1.0 scatter_custom_fusion
  139.3 1.2 gather_fusion.2
  140.5 10.1 %gather_fusion.3 = bf16[128,28,1024]{2,1,0:T(8,128)(2,1)} fusion(bf16[128,28,1024]{2,1,0:T(8,128)(2,1)} %bitcast.6, s32[1024]{0:T(1024)S(1)} %pad_clamp_fusion), kind=kCustom, calls=%fused_computation.3 | custom fusion | bytes 14680576 | tf_op jit(solution)/shard_map/jit(_take)/gather | solution.py:72
  150.6 7.5 %broadcast_select_fusion = bf16[128,28,1024]{2,1,0:T(8,128)(2,1)} fusion(bf16[128,28,1024]{2,1,0:T(8,128)(2,1)} %gather_fusion.3, pred[128]{0:T(512)(128)(4,1)S(1)} %compare_and_fusion), kind=kLoop, calls=%fused_computation.6 | loop fusion | flops 3670016 | bytes 14680192 | tf_op jit(solution)/shard_map/jit(_take)/select_n | solution.py:72
  158.2 179.7 %all-to-all-done = bf16[2,128,28,1024]{3,0,2,1:T(2,128)(2,1)} async-done(((bf16[2,128,28,1024]{3,0,2,1:T(2,128)(2,1)}), bf16[2,128,28,1024]{3,0,2,1:T(2,128)(2,1)}, u32[]{:S(2)}, u32[]{:S(2)}) %all-to-all-start) | async-done | bytes 14680096 | tf_op jit(solution)/shard_map/all_to_all | solution.py:60
  337.9 12.2 %all-to-all-start.3 = ((bf16[128,28,1024]{2,1,0:T(8,128)(2,1)}), bf16[128,28,1024]{2,1,0:T(8,128)(2,1)}, u32[]{:S(2)}, u32[]{:S(2)}) async-start(bf16[128,28,1024]{2,1,0:T(8,128)(2,1)} %broadcast_select_fusion), calls=%async_computation.3 | async-start | bytes 16777216 | tf_op jit(solution)/shard_map/all_to_all | solution.py:76
  350.1 0.0 copy-done.2
  350.1 1.2 gather_fusion
  351.4 15.6 %copy.49 = bf16[2,128,28,1024]{3,2,1,0:T(8,128)(2,1)} copy(bf16[2,128,28,1024]{3,0,2,1:T(2,128)(2,1)} %all-to-all-done) | data formatting | bytes 29360128 | tf_op jit(solution)/shard_map/reshape | solution.py:69
  367.0 12.3 %gather_fusion.1 = bf16[128,28,1024]{2,1,0:T(8,128)(2,1)} fusion(bf16[256,28,1024]{2,1,0:T(8,128)(2,1)} %bitcast.114, s32[1024]{0:T(1024)S(1)} %pad_clamp_fusion.1), kind=kCustom, calls=%fused_computation.1 | custom fusion | bytes 14680576 | tf_op jit(solution)/shard_map/jit(_take)/gather | solution.py:74
  379.4 7.4 broadcast_select_fusion.1
  386.8 69.8 %all-to-all-done.3 = bf16[128,28,1024]{2,1,0:T(8,128)(2,1)} async-done(((bf16[128,28,1024]{2,1,0:T(8,128)(2,1)}), bf16[128,28,1024]{2,1,0:T(8,128)(2,1)}, u32[]{:S(2)}, u32[]{:S(2)}) %all-to-all-start.3) | async-done | bytes 7340064 | tf_op jit(solution)/shard_map/all_to_all | solution.py:76
  456.6 106.2 %all_to_all.20 = bf16[128,28,1024]{2,1,0:T(8,128)(2,1)S(1)} all-to-all(bf16[128,28,1024]{2,1,0:T(8,128)(2,1)} %broadcast_select_fusion.1), channel_id=1, replica_groups=mesh['grp'=4,'ep'=32] {'grp','ep'}, dimensions={0} | all-to-all | bytes 14680064 | tf_op jit(solution)/shard_map/all_to_all | solution.py:77
  562.8 9.0 %subtract_convert_fusion = bf16[128,28,1024]{2,1,0:T(8,128)(2,1)} fusion(bf16[128,28,1024]{2,1,0:T(8,128)(2,1)} %all-to-all-done.3, bf16[128,28,1024]{2,1,0:T(8,128)(2,1)S(1)} %all_to_all.20), kind=kLoop, calls=%fused_computation.5 | loop fusion | flops 14680064 | bytes 22020096 | tf_op jit(solution)/shard_map/convert_element_type | solution.py:82
  571.8 11.4 %convert_element_type.37 = bf16[3584,1024]{1,0:T(8,128)(2,1)} reshape(bf16[128,28,1024]{2,1,0:T(8,128)(2,1)} %subtract_convert_fusion) | data formatting | bytes 14680064 | tf_op jit(solution)/shard_map/convert_element_type | solution.py:82
  583.2 5.1 fusion.38
  588.3 3.0 fusion.39
  591.4 0.1 copy.43
  591.5 11.7 %cholesky.89 = f32[128,128]{1,0:T(8,128)S(1)} custom-call(f32[128,128]{1,0:T(8,128)S(1)} %fusion.21), custom_call_target="Cholesky" | custom-call | tf_op jit(solution)/shard_map/jit(cholesky)/cholesky | solution.py:22
  603.2 0.6 compare_reduce_fusion.4
  603.9 0.7 fusion.7
  604.6 9.8 %custom-call.11 = f32[1,128,128]{1,2,0:T(8,128)S(1)} custom-call(f32[1,128,128]{2,1,0:T(8,128)S(1)} %fusion.7), custom_call_target="InvertDiagBlocksLowerTriangular" | custom-call | tf_op jit(solution)/shard_map/jit(_solve_triangular)/triangular_solve | solution.py:23
  614.4 1.9 convolution_convert_fusion.1
  616.3 5.2 fusion.40
  621.5 1.0 fusion.41
  622.5 0.1 copy.44
  622.6 11.7 %cholesky.100 = f32[128,128]{1,0:T(8,128)S(1)} custom-call(f32[128,128]{1,0:T(8,128)S(1)} %fusion.19), custom_call_target="Cholesky" | custom-call | tf_op jit(solution)/shard_map/jit(cholesky)/cholesky | solution.py:22
  634.4 0.6 compare_reduce_fusion.3
  635.0 0.7 fusion.8
  635.7 9.8 %custom-call.12 = f32[1,128,128]{1,2,0:T(8,128)S(1)} custom-call(f32[1,128,128]{2,1,0:T(8,128)S(1)} %fusion.8), custom_call_target="InvertDiagBlocksLowerTriangular" | custom-call | tf_op jit(solution)/shard_map/jit(_solve_triangular)/triangular_solve | solution.py:23
  645.5 0.6 convolution_convert_fusion.3
  646.1 5.4 fusion.42
  651.5 3.0 fusion.43
  654.6 0.1 copy.45
  654.7 11.7 %cholesky.111 = f32[128,128]{1,0:T(8,128)S(1)} custom-call(f32[128,128]{1,0:T(8,128)S(1)} %fusion.17), custom_call_target="Cholesky" | custom-call | tf_op jit(solution)/shard_map/jit(cholesky)/cholesky | solution.py:22
  666.4 0.6 compare_reduce_fusion.2
  667.1 0.7 fusion.9
  667.7 9.8 %custom-call.13 = f32[1,128,128]{1,2,0:T(8,128)S(1)} custom-call(f32[1,128,128]{2,1,0:T(8,128)S(1)} %fusion.9), custom_call_target="InvertDiagBlocksLowerTriangular" | custom-call | tf_op jit(solution)/shard_map/jit(_solve_triangular)/triangular_solve | solution.py:23
  677.6 1.7 convolution_convert_fusion
  679.3 5.6 fusion.44
  684.9 1.0 fusion.45
  685.9 0.1 copy.46
  686.0 11.7 %cholesky.122 = f32[128,128]{1,0:T(8,128)S(1)} custom-call(f32[128,128]{1,0:T(8,128)S(1)} %fusion.15), custom_call_target="Cholesky" | custom-call | tf_op jit(solution)/shard_map/jit(cholesky)/cholesky | solution.py:22
  697.8 0.6 compare_reduce_fusion.1
  698.4 0.7 fusion.10
  699.1 9.8 %custom-call.14 = f32[1,128,128]{1,2,0:T(8,128)S(1)} custom-call(f32[1,128,128]{2,1,0:T(8,128)S(1)} %fusion.10), custom_call_target="InvertDiagBlocksLowerTriangular" | custom-call | tf_op jit(solution)/shard_map/jit(_solve_triangular)/triangular_solve | solution.py:23
  708.9 0.6 convolution_convert_fusion.2
  709.5 5.2 fusion.46
  714.7 3.2 fusion.47
  717.9 0.1 copy.47
  718.0 11.7 %cholesky.133 = f32[128,128]{1,0:T(8,128)S(1)} custom-call(f32[128,128]{1,0:T(8,128)S(1)} %fusion.13), custom_call_target="Cholesky" | custom-call | tf_op jit(solution)/shard_map/jit(cholesky)/cholesky | solution.py:22
  729.8 0.6 compare_reduce_fusion
  730.4 0.7 fusion.11
  731.1 9.8 %custom-call.15 = f32[1,128,128]{1,2,0:T(8,128)S(1)} custom-call(f32[1,128,128]{2,1,0:T(8,128)S(1)} %fusion.11), custom_call_target="InvertDiagBlocksLowerTriangular" | custom-call | tf_op jit(solution)/shard_map/jit(_solve_triangular)/triangular_solve | solution.py:23
  740.9 1.7 fusion
  742.6 5.1 convolution_bitcast_fusion
  747.7 0.2 multiply_bitcast_fusion
  747.9 1.7 copy.48
  (26 shorter events, 0.3 us)
Async XLA Ops:
  0.6 582.5 %copy-start = (bf16[1024,128]{1,0:T(8,128)(2,1)S(1)}, bf16[1024,128]{1,0:T(8,128)(2,1)}, u32[]{:S(2)}) copy-start(bf16[1024,128]{1,0:T(8,128)(2,1)} %param.13) | copy-start | bytes 786436
  11.6 118.4 %all-to-all-start.2 = ((bf16[1,128,28,1024]{3,2,0,1:T(8,128)(2,1)}), bf16[1,128,28,1024]{3,2,0,1:T(8,128)(2,1)}, u32[]{:S(2)}, u32[]{:S(2)}) async-start(bf16[1,128,28,1024]{3,2,0,1:T(8,128)(2,1)} %bitcast.115), calls=%async_computation.2 | async-start | bytes 16777216 | tf_op jit(solution)/shard_map/all_to_all | solution.py:53
  130.0 8.2 %copy-start.3 = (s32[128]{0:T(128)S(1)}, s32[128]{0:T(128)}, u32[]{:S(2)}) copy-start(s32[128]{0:T(128)} %param.16) | copy-start | bytes 1540
  130.0 9.3 %copy-start.1 = (s32[128]{0:T(128)S(1)}, s32[128]{0:T(128)}, u32[]{:S(2)}) copy-start(s32[128]{0:T(128)} %param.14) | copy-start | bytes 1540
  130.0 207.9 %all-to-all-start = ((bf16[2,128,28,1024]{3,0,2,1:T(2,128)(2,1)}), bf16[2,128,28,1024]{3,0,2,1:T(2,128)(2,1)}, u32[]{:S(2)}, u32[]{:S(2)}) async-start(bf16[2,128,28,1024]{3,0,2,1:T(2,128)(2,1)} %bitcast.113), calls=%async_computation | async-start | bytes 29360128 | tf_op jit(solution)/shard_map/all_to_all | solution.py:60
  158.2 192.0 %copy-start.2 = (s32[128]{0:T(128)S(1)}, s32[128]{0:T(128)}, u32[]{:S(2)}) copy-start(s32[128]{0:T(128)} %param.15) | copy-start | bytes 1540
  337.9 118.7 %all-to-all-start.3 = ((bf16[128,28,1024]{2,1,0:T(8,128)(2,1)}), bf16[128,28,1024]{2,1,0:T(8,128)(2,1)}, u32[]{:S(2)}, u32[]{:S(2)}) async-start(bf16[128,28,1024]{2,1,0:T(8,128)(2,1)} %broadcast_select_fusion), calls=%async_computation.3 | async-start | bytes 16777216 | tf_op jit(solution)/shard_map/all_to_all | solution.py:76
where the time goes:
time: 760 us; the launch traced here: 750 us
  waiting for transfers between devices  329 us (43%)
  other arithmetic  138 us (18%)
  blocking collectives  106 us (14%)
  local copies, waits for them, and re-layouts  93.3 us (12%)
  matrix products  49.6 us (7%)
  starting transfers between devices  32.4 us (4%)
    all_to_all x1, waiting for transfers between devices, shards(): lax.all_to_all(adjusted_tiles.reshape(2, count, piece, width), ('grp', 'e...  180 us
    all_to_all x1, blocking collectives, shards(): lax.all_to_all(adjusted_rows, ('grp', 'ep'), split_axis=0, concat_axis=0,...  106 us
    all_to_all x1, waiting for transfers between devices, shards(): lax.all_to_all(base_tiles.reshape(1, count, piece, width), ('grp', 'ep'),...  79.1 us
    all_to_all x1, waiting for transfers between devices, shards(): lax.all_to_all(base_rows, ('grp', 'ep'), split_axis=0, concat_axis=0, til...  69.8 us
    another operation x15, other arithmetic, orthonormal(): factor_low = jnp.linalg.cholesky(gram_matrix)  61.9 us
    another operation x10, other arithmetic, orthonormal(): jax.scipy.linalg.solve_triangular(factor_low, columns.T, lower=True)  52.3 us
    unnamed x10, local copies, waits for them, and re-layouts  29 us
    reshape x1, local copies, waits for them, and re-layouts, shards(): adjusted_flat = adjusted_got.reshape(2 * count, piece, width)  15.6 us
  transfers between devices with their start and end apart: 3, of which 3 were waited for; matrix products, arithmetic and copies ran while one was open for 11% of the time, Pallas kernels for 0%

commit v1 on v0

v1 whole, which is shorter than its diff:
```python
import functools
import math

import jax
import jax.numpy as jnp
from jax import lax
from jax.experimental import pallas as pl
from jax.experimental.pallas import tpu as pltpu
from jax.sharding import PartitionSpec as P

MESH = pl.DeviceIdType.MESH
N = 128
HI = lax.Precision.HIGHEST
F32=jnp.float32; BF=jnp.bfloat16
NT = (((1,),(1,)),((),()))
NN = (((1,),(0,)),((),()))
TN = (((0,),(0,)),((),()))
K=128; C=512; NC=7

def dot(a,b,dims,precision=None):
    return lax.dot_general(a,b,dims,precision=precision,preferred_element_type=F32)

def chol_inv(g_ref, m_ref, w_ref):
    sub = lax.broadcasted_iota(jnp.int32, (8,128), 0)
    a = g_ref[...]
    row = lax.broadcasted_iota(jnp.int32, (K,K), 0); col = lax.broadcasted_iota(jnp.int32, (K,K), 1)
    x = jnp.where(row==col, 1.0, 0.0).astype(F32)
    for j in range(16):
        r0 = 8*j
        p = a[:8]; xp = x[:8]
        s = {}
        for i in range(8):
            for k in range(i+1):
                s[i,k] = jnp.broadcast_to(p[i:i+1, r0+k:r0+k+1], (8,128))
        rows = [jnp.broadcast_to(p[i:i+1,:],(8,128)) for i in range(8)]
        xrows = [jnp.broadcast_to(xp[i:i+1,:],(8,128)) for i in range(8)]
        u = None; w = None
        for k in range(8):
            v = s[k,k]
            r = lax.rsqrt(v)
            uk = rows[k]*r; wk = xrows[k]*r
            u = uk if k==0 else jnp.where(sub==k, uk, u)
            w = wk if k==0 else jnp.where(sub==k, wk, w)
            l = {i: s[i,k]*r for i in range(k+1,8)}
            for i in range(k+1,8):
                for m in range(k+1,i+1):
                    s[i,m] = s[i,m]-l[i]*l[m]
            for i in range(k+1,8):
                rows[i] = rows[i]-l[i]*uk
                xrows[i] = xrows[i]-l[i]*wk
        w_ref[pl.ds(r0,8),:] = w
        if j<15:
            upd = dot(u, jnp.concatenate([u,w],axis=1), TN, HI)
            a = a[8:] - upd[r0+8:, :K]
            x = x[8:] - upd[r0+8:, K:]

def k2_kernel(adj_ref, base_ref, s_ref, out_ref, d, yt, zt, g, m, w, ab, bb, asem, bsem):
    def ca(c): return pltpu.make_async_copy(adj_ref.at[pl.ds(c*C,C)], ab.at[c], asem.at[c])
    def cb(c): return pltpu.make_async_copy(base_ref.at[pl.ds(c*C,C)], bb.at[c], bsem.at[c])
    for c in range(NC):
        ca(c).start(); cb(c).start()
    st = s_ref[...].astype(F32).T.astype(BF)
    g[...] = jnp.zeros_like(g)
    def first(c, car):
        ca(c).wait(); cb(c).wait()
        dc = (ab[c].astype(F32)-bb[c].astype(F32)).astype(BF)
        d[c] = dc
        y = dot(st, dc, NT)
        yt[c] = y
        g[...] += dot(y, y, NT, HI)
        return car
    lax.fori_loop(0,NC,first,0)
    def step(t, car):
        chol_inv(g, m, w)
        @pl.when(t%2==0)
        def _():
            zt[...] = jnp.zeros_like(zt)
            wv = w[...]
            def app(c, car):
                q = dot(wv, yt[c], NN, HI)
                qb = q.astype(BF)
                zt[...] += dot(qb, d[c], NN)
                @pl.when(t==4)
                def _():
                    out_ref[pl.ds(pl.multiple_of(c*C,C),C),:] = q.T.astype(BF)
                return car
            lax.fori_loop(0,NC,app,0)
            z = zt[...]
            g[...] = dot(z,z,NT,HI)
            @pl.when(t==4)
            def _():
                for j in range(8):
                    out_ref[3584+128*j:3584+128*(j+1),:] = zt[:,128*j:128*(j+1)].astype(BF)
        @pl.when(t%2==1)
        def _():
            at = dot(w[...], zt[...], NN, HI).astype(BF)
            g[...] = jnp.zeros_like(g)
            def back(c, car):
                y = dot(at, d[c], NT)
                yt[c] = y
                g[...] += dot(y,y,NT,HI)
                return car
            lax.fori_loop(0,NC,back,0)
        return car
    lax.fori_loop(0,5,step,0)

def k2(adj, base, sketch):
    return pl.pallas_call(k2_kernel,
        out_shape=jax.ShapeDtypeStruct((6144,128),BF),
        in_specs=[pl.BlockSpec(memory_space=pl.ANY)]*2+[pl.BlockSpec(memory_space=pltpu.VMEM)],
        out_specs=pl.BlockSpec(memory_space=pltpu.VMEM),
        scratch_shapes=[pltpu.VMEM((NC,C,1024),BF), pltpu.VMEM((NC,K,C),F32), pltpu.VMEM((K,1024),F32),
          pltpu.VMEM((K,K),F32), pltpu.VMEM((K,2*K),F32), pltpu.VMEM((K,K),F32),
          pltpu.VMEM((NC,C,1024),BF), pltpu.VMEM((NC,C,1024),BF), pltpu.SemaphoreType.DMA((NC,)), pltpu.SemaphoreType.DMA((NC,))],
        compiler_params=pltpu.CompilerParams(vmem_limit_bytes=48*2**20), name="factor")(adj,base,sketch)


def peer(o):
    x = lax.axis_index("grp")
    e = lax.axis_index("ep")
    o = (o * 37) % 128
    tx = (x + o // 32) % 4
    tz = (e // 8 + (o // 8) % 4) % 4
    ty = ((e // 2) % 4 + (o // 2) % 4) % 4
    tc = (e + o) % 2
    return tx, tz * 8 + ty * 2 + tc


def route_kernel(src_block, dst_block, slots, idx_ref, src_ref, dst_ref, got, out, ssem, rsem, s2sem, r2sem, lsem, l2sem):
    x = lax.axis_index("grp")
    e = lax.axis_index("ep")
    me = x * 32 + e
    mine = pl.ds(slots * me, slots)
    own = pltpu.make_async_copy(src_block(src_ref, me), got.at[mine], lsem)
    own.start()

    def spread(o, car):
        tx, te = peer(o)
        pltpu.make_async_remote_copy(
            src_block(src_ref, tx * 32 + te), got.at[mine], ssem, rsem, device_id=(tx, te), device_id_type=MESH
        ).start()
        return car

    lax.fori_loop(1, N, spread, 0)
    own.wait()
    most = got.at[pl.ds(0, slots * (N - 1))]
    pltpu.make_async_copy(most, most, rsem).wait()

    def pick(b, car):
        out[b] = got[idx_ref[b]]
        return car

    lax.fori_loop(0, N, pick, 0)
    own2 = pltpu.make_async_copy(out.at[me], dst_block(dst_ref, me), l2sem)
    own2.start()

    def collect(o, car):
        tx, te = peer(o)
        pltpu.make_async_remote_copy(
            out.at[tx * 32 + te], dst_block(dst_ref, me), s2sem, r2sem, device_id=(tx, te), device_id_type=MESH
        ).start()
        return car

    lax.fori_loop(1, N, collect, 0)
    pltpu.make_async_copy(most, most, ssem).wait()
    own2.wait()
    rest = out.at[pl.ds(0, N - 1)]
    pltpu.make_async_copy(rest, rest, r2sem).wait()
    pltpu.make_async_copy(rest, rest, s2sem).wait()


def route(src_block, dst_block, slots, piece, idx, src, shape, name):
    return pl.pallas_call(
        functools.partial(route_kernel, src_block, dst_block, slots),
        out_shape=jax.ShapeDtypeStruct(shape, BF),
        in_specs=[pl.BlockSpec(memory_space=pltpu.SMEM), pl.BlockSpec(memory_space=pl.ANY)],
        out_specs=pl.BlockSpec(memory_space=pl.ANY),
        scratch_shapes=[pltpu.VMEM((slots * N,) + piece, BF), pltpu.VMEM((N,) + piece, BF)]
        + [pltpu.SemaphoreType.DMA] * 6,
        compiler_params=pltpu.CompilerParams(has_side_effects=True, vmem_limit_bytes=48 * 2**20),
        name=name,
    )(idx, src)


def tile_rows(i):
    return pl.ds(pl.multiple_of((i // 4) * 112, 112), 112)


def tile_columns(i):
    return pl.ds(pl.multiple_of((i % 4) * 256, 256), 256)


def both_slots(ref, i):
    return ref.at[:, tile_rows(i), tile_columns(i)]


def one_tile(ref, i):
    return ref.at[tile_rows(i), tile_columns(i)]


def result_rows(ref, i):
    return ref.at[pl.ds(pl.multiple_of(i * 48, 48), 48)]


def result_rows_in(ref, i):
    return ref.at[pl.ds(0, 1), pl.ds(pl.multiple_of(i * 48, 48), 48)]


def by_key(key, value):
    places = lax.broadcasted_iota(jnp.int32, (N, N), 0)
    return jnp.sum(jnp.where(places == key[None, :], value[None, :], 0), axis=1, dtype=jnp.int32)


def shards(base_tiles, adjusted_tiles, sketch, base_place, adjusted_place, owner_map):
    adjusted_of = by_key(base_place, adjusted_place)
    result_of = by_key(owner_map, base_place)
    adjusted = route(both_slots, one_tile, 2, (112, 256), adjusted_of, adjusted_tiles, (3584, 1024), "move_adjusted")
    result = k2(adjusted, base_tiles[0], sketch)
    moved = route(result_rows_in, result_rows, 1, (48, 128), result_of, result[None], (6144, 128), "move_result")
    scaled_basis = moved[:3584].astype(F32) * math.sqrt(3584)
    projected = moved[3584:4608].astype(F32).reshape(8, 128, 128).transpose(1, 0, 2).reshape(128, 1024)
    return (scaled_basis[None], projected[None])


def solution(mesh):
    in_specs = (P(("grp", "ep"), None, None), P(("grp", "ep"), None, None), P(), P(), P(), P())
    out_specs = (P(("grp", "ep"), None, None), P(("grp", "ep"), None, None))
    return jax.shard_map(shards, mesh=mesh, in_specs=in_specs, out_specs=out_specs, check_vma=False)
```

time: 760 us -> 474 us (0.62); the launches traced: 750 us -> 474 us
  Pallas kernels: 0 us -> 470 us
  waiting for transfers between devices: 329 us -> 0 us
  other arithmetic: 138 us -> 2.2 us
  blocking collectives: 106 us -> 0 us
  local copies, waits for them, and re-layouts: 93.3 us -> 1.21 us
  matrix products: 49.6 us -> 0 us
  starting transfers between devices: 32.4 us -> 0 us
    pallas_call x0 -> x3, Pallas kernels: none -> 470 us  [the longest x2 390 us: route(): pl.pallas_call(functools.partial(route_kernel, src_block, dst_block, slot...]
    all_to_all x3 -> x0, waiting for transfers between devices: 329 us -> none  [the longest x1 180 us: shards(): lax.all_to_all(adjusted_tiles.reshape(2, count, piece, width), ('grp', 'e...]
    another operation x25 -> x1, other arithmetic: 114 us -> 0.04 us  [shards(): return (scaled_basis[None], projected[None])]
    all_to_all x1 -> x0, blocking collectives: 106 us -> none  [shards(): lax.all_to_all(adjusted_rows, ('grp', 'ep'), split_axis=0, concat_axis=0,...]
    dot_general x11 -> x0, matrix products: 42.9 us -> none  [the longest x5 11.3 us: orthonormal(): lax.dot_general(columns, columns, (((0,), (0,)), ((), ())), precision=hig...]
    all_to_all x3 -> x0, starting transfers between devices: 32.4 us -> none  [the longest x1 12.2 us: shards(): lax.all_to_all(base_rows, ('grp', 'ep'), split_axis=0, concat_axis=0, til...]
    unnamed x10 -> x2, local copies, waits for them, and re-layouts: 29 us -> 0.01 us
    reshape x2 -> x0, local copies, waits for them, and re-layouts: 26.6 us -> none  [the longest x1 15.6 us: shards(): adjusted_flat = adjusted_got.reshape(2 * count, piece, width)]
  transfers between devices with their start and end apart: 3 -> 0, of which waited for: 3 -> 0; matrix products, arithmetic and copies ran while one was open for 11% -> 0% of each run, Pallas kernels for 0% -> 0%
where the time goes in v1:
time: 474 us
  Pallas kernels  470 us (99%)
    pallas_call x2, Pallas kernels, route(): pl.pallas_call(functools.partial(route_kernel, src_block, dst_block, slot...  390 us
    pallas_call x1, Pallas kernels, k2(): pl.pallas_call(k2_kernel, out_shape=jax.ShapeDtypeStruct((6144, 128), BF)...  80.2 us

profile of v1, /device:TPU:1, one launch (start us, length us, event | category | flops | bytes accessed | tf_op | source)
XLA Modules:
  0.0 474.3 jit_solution(1369060161238739077)
XLA Ops:
  0.6 0.8 select_reduce_fusion
  1.4 0.0 copy-start
  1.4 319.0 %move_adjusted.1.adj_ref = bf16[3584,1024]{1,0:T(8,128)(2,1)} custom-call(s32[128]{0:T(128)S(1)} %get-tuple-element.2.idx_ref, bf16[2,3584,1024]{2,1,0:T(8,128)(2,1)} %src_ref.1), custom_call_target="tpu_custom_call" | custom-call | tf_op jit(solution)/shard_map/move_adjusted/pallas_call | solution.py:173
  320.4 0.0 copy-done
  320.5 80.2 %factor.1 = bf16[6144,128]{1,0:T(8,128)(2,1)S(1)} custom-call(bf16[3584,1024]{1,0:T(8,128)(2,1)} %move_adjusted.1.adj_ref, bf16[3584,1024]{1,0:T(8,128)(2,1)} %bitcast.9, bf16[1024,128]{1,0:T(8,128)(2,1)S(1)} %copy-done), custom_call_target="tpu_custom_call" | custom-call | tf_op jit(solution)/shard_map/factor/pallas_call | solution.py:108
  400.7 71.0 %move_result.1 = bf16[6144,128]{1,0:T(8,128)(2,1)S(1)} custom-call(s32[128]{0:T(128)S(1)} %get-tuple-element.3.idx_ref, bf16[1,6144,128]{2,1,0:T(8,128)(2,1)S(1)} %bitcast.8), custom_call_target="tpu_custom_call" | custom-call | tf_op jit(solution)/shard_map/move_result/pallas_call | solution.py:173
  471.8 0.3 copy.9
  472.1 0.9 reshape.12
  473.0 1.4 multiply_bitcast_fusion
  (2 shorter events, 0.1 us)
Async XLA Ops:
  1.4 319.0 %copy-start = (bf16[1024,128]{1,0:T(8,128)(2,1)S(1)}, bf16[1024,128]{1,0:T(8,128)(2,1)}, u32[]{:S(2)}) copy-start(bf16[1024,128]{1,0:T(8,128)(2,1)} %s_ref.1) | copy-start | bytes 786436

commit v2 on v1

v2 whole, which is shorter than its diff:
```python
import functools
import math

import jax
import jax.numpy as jnp
from jax import lax
from jax.experimental import pallas as pl
from jax.experimental.pallas import tpu as pltpu
from jax.sharding import PartitionSpec as P

MESH = pl.DeviceIdType.MESH
N = 128
F32=jnp.float32; BF=jnp.bfloat16
NT = (((1,),(1,)),((),()))
NN = (((1,),(0,)),((),()))
TN = (((0,),(0,)),((),()))
K=128; C=512; NC=7

def dot(a,b,dims,precision=None):
    return lax.dot_general(a,b,dims,precision=precision,preferred_element_type=F32)

def split3(v):
    hi = v.astype(BF).astype(F32)
    rest = v - hi
    mid = rest.astype(BF).astype(F32)
    return hi, mid, rest - mid


def chol_inv(g_ref, w_ref):
    sub = lax.broadcasted_iota(jnp.int32, (8, K), 0)
    a = g_ref[...]
    row = lax.broadcasted_iota(jnp.int32, (K, K), 0)
    col = lax.broadcasted_iota(jnp.int32, (K, K), 1)
    x = jnp.where(row == col, 1.0, 0.0).astype(F32)
    for r0 in range(0, K, 8):
        p = a[:8]
        xp = x[:8]
        s = {}
        for i in range(8):
            for k in range(i + 1):
                s[i, k] = jnp.broadcast_to(p[i : i + 1, r0 + k : r0 + k + 1], (8, K))
        rows = [jnp.broadcast_to(p[i : i + 1, :], (8, K)) for i in range(8)]
        xrows = [jnp.broadcast_to(xp[i : i + 1, :], (8, K)) for i in range(8)]
        u = jnp.zeros((8, K), F32)
        w = jnp.zeros((8, K), F32)
        for k in range(8):
            r = lax.rsqrt(s[k, k])
            uk = rows[k] * r
            wk = xrows[k] * r
            u = jnp.where(sub == k, uk, u)
            w = jnp.where(sub == k, wk, w)
            l = {i: s[i, k] * r for i in range(k + 1, 8)}
            for i in range(k + 1, 8):
                for m in range(k + 1, i + 1):
                    s[i, m] = s[i, m] - l[i] * l[m]
            for i in range(k + 1, 8):
                rows[i] = rows[i] - l[i] * uk
                xrows[i] = xrows[i] - l[i] * wk
        w_ref[pl.ds(r0, 8), :] = w
        if r0 < K - 8:
            uh, um, ul = split3(u)
            wh, wm, wl = split3(w)
            left = jnp.concatenate([uh, uh, um, uh, ul, um], axis=0).astype(BF)
            right = jnp.concatenate(
                [
                    jnp.concatenate([uh, um, uh, ul, uh, um], axis=0).astype(BF),
                    jnp.concatenate([wh, wm, wh, wl, wh, wm], axis=0).astype(BF),
                ],
                axis=1,
            )
            upd = dot(left, right, TN)
            a = a[8:] - upd[r0 + 8 :, :K]
            x = x[8:] - upd[r0 + 8 :, K:]


def wide_left(v):
    hi = v.astype(BF)
    return jnp.concatenate([hi, hi, (v - hi.astype(F32)).astype(BF)], axis=1)


def wide_right(v):
    hi = v.astype(BF)
    return jnp.concatenate([hi, (v - hi.astype(F32)).astype(BF), hi], axis=0)


def gram(v):
    hi, mid, low = (part.astype(BF) for part in split3(v))
    first = dot(hi, jnp.concatenate([hi, mid, low], axis=0), NT)
    cross = first[:, K : 2 * K] + first[:, 2 * K :]
    return first[:, :K] + dot(mid, mid, NT) + cross + cross.T


def k2_kernel(adj_ref, base_ref, s_ref, out_ref, d, yt, zt, g, w, ab, bb, asem, bsem):
    def ca(c): return pltpu.make_async_copy(adj_ref.at[pl.ds(c*C,C)], ab.at[c], asem.at[c])
    def cb(c): return pltpu.make_async_copy(base_ref.at[pl.ds(c*C,C)], bb.at[c], bsem.at[c])
    for c in range(NC):
        ca(c).start(); cb(c).start()
    st = s_ref[...].astype(F32).T.astype(BF)
    g[...] = jnp.zeros_like(g)
    def first(c, car):
        ca(c).wait(); cb(c).wait()
        dc = (ab[c].astype(F32)-bb[c].astype(F32)).astype(BF)
        d[c] = dc
        y = dot(st, dc, NT)
        yt[c] = y
        g[...] += gram(y)
        return car
    lax.fori_loop(0,NC,first,0)
    def step(t, car):
        chol_inv(g, w)
        @pl.when(t%2==0)
        def _():
            zt[...] = jnp.zeros_like(zt)
            wv = wide_left(w[...])
            def app(c, car):
                q = dot(wv, wide_right(yt[c]), NN)
                qb = q.astype(BF)
                zt[...] += dot(qb, d[c], NN)
                @pl.when(t==4)
                def _():
                    out_ref[pl.ds(pl.multiple_of(c*C,C),C),:] = q.T.astype(BF)
                return car
            lax.fori_loop(0,NC,app,0)
            z = zt[...]
            g[...] = gram(z)
            @pl.when(t==4)
            def _():
                for j in range(8):
                    out_ref[3584+128*j:3584+128*(j+1),:] = zt[:,128*j:128*(j+1)].astype(BF)
        @pl.when(t%2==1)
        def _():
            at = dot(wide_left(w[...]), wide_right(zt[...]), NN).astype(BF)
            g[...] = jnp.zeros_like(g)
            def back(c, car):
                y = dot(at, d[c], NT)
                yt[c] = y
                g[...] += gram(y)
                return car
            lax.fori_loop(0,NC,back,0)
        return car
    lax.fori_loop(0,5,step,0)

def k2(adj, base, sketch):
    return pl.pallas_call(k2_kernel,
        out_shape=jax.ShapeDtypeStruct((6144,128),BF),
        in_specs=[pl.BlockSpec(memory_space=pl.ANY)]*2+[pl.BlockSpec(memory_space=pltpu.VMEM)],
        out_specs=pl.BlockSpec(memory_space=pltpu.VMEM),
        scratch_shapes=[pltpu.VMEM((NC,C,1024),BF), pltpu.VMEM((NC,K,C),F32), pltpu.VMEM((K,1024),F32),
          pltpu.VMEM((K,K),F32), pltpu.VMEM((K,K),F32),
          pltpu.VMEM((NC,C,1024),BF), pltpu.VMEM((NC,C,1024),BF), pltpu.SemaphoreType.DMA((NC,)), pltpu.SemaphoreType.DMA((NC,))],
        compiler_params=pltpu.CompilerParams(vmem_limit_bytes=48*2**20), name="factor")(adj,base,sketch)


def peer(o):
    x = lax.axis_index("grp")
    e = lax.axis_index("ep")
    o = (o * 101) % 128
    sign = 1 - 2 * (e % 2)
    tx = (x + 4 + sign * (o // 32)) % 4
    tz = (e // 8 + 4 + sign * ((o // 8) % 4)) % 4
    ty = ((e // 2) % 4 + 4 + sign * ((o // 2) % 4)) % 4
    return tx, tz * 8 + ty * 2 + (e + o) % 2


def route_kernel(src_block, dst_block, slots, chunks, idx_ref, src_ref, dst_ref, *scratch):
    parts = len(chunks)
    gots = scratch[:parts]
    outs = scratch[parts : 2 * parts]
    ssem, rsem, s2sem, r2sem, lsem, l2sem = scratch[2 * parts :]
    me = lax.axis_index("grp") * 32 + lax.axis_index("ep")
    mine = pl.ds(slots * me, slots)

    def own(k):
        return pltpu.make_async_copy(src_block(src_ref, me, *chunks[k]), gots[k].at[mine], lsem.at[k])

    def own2(k):
        return pltpu.make_async_copy(outs[k].at[me], dst_block(dst_ref, me, *chunks[k]), l2sem.at[k])

    for k in range(parts):
        own(k).start()

        def spread(o, car, k=k):
            tx, te = peer(o)
            pltpu.make_async_remote_copy(
                src_block(src_ref, tx * 32 + te, *chunks[k]),
                gots[k].at[mine],
                ssem.at[k],
                rsem.at[k],
                device_id=(tx, te),
                device_id_type=MESH,
            ).start()
            return car

        lax.fori_loop(1, N, spread, 0)
    for k in range(parts):
        own(k).wait()
        most = gots[k].at[pl.ds(0, slots * (N - 1))]
        pltpu.make_async_copy(most, most, rsem.at[k]).wait()

        def pick(b, car, k=k):
            outs[k][b] = gots[k][idx_ref[b]]
            return car

        lax.fori_loop(0, N, pick, 0)
        own2(k).start()

        def collect(o, car, k=k):
            tx, te = peer(o)
            pltpu.make_async_remote_copy(
                outs[k].at[tx * 32 + te],
                dst_block(dst_ref, me, *chunks[k]),
                s2sem.at[k],
                r2sem.at[k],
                device_id=(tx, te),
                device_id_type=MESH,
            ).start()
            return car

        lax.fori_loop(1, N, collect, 0)
    for k in range(parts):
        own2(k).wait()
        most = gots[k].at[pl.ds(0, slots * (N - 1))]
        pltpu.make_async_copy(most, most, ssem.at[k]).wait()
        rest = outs[k].at[pl.ds(0, N - 1)]
        pltpu.make_async_copy(rest, rest, r2sem.at[k]).wait()
        pltpu.make_async_copy(rest, rest, s2sem.at[k]).wait()


def route(src_block, dst_block, slots, columns, chunks, idx, src, shape, name):
    return pl.pallas_call(
        functools.partial(route_kernel, src_block, dst_block, slots, chunks),
        out_shape=jax.ShapeDtypeStruct(shape, BF),
        in_specs=[pl.BlockSpec(memory_space=pltpu.SMEM), pl.BlockSpec(memory_space=pl.ANY)],
        out_specs=pl.BlockSpec(memory_space=pl.ANY),
        scratch_shapes=[pltpu.VMEM((slots * N, rows, columns), BF) for _, rows in chunks]
        + [pltpu.VMEM((N, rows, columns), BF) for _, rows in chunks]
        + [pltpu.SemaphoreType.DMA((len(chunks),))] * 6,
        compiler_params=pltpu.CompilerParams(has_side_effects=True, vmem_limit_bytes=48 * 2**20),
        name=name,
    )(idx, src)


def tile(i, first, rows):
    return pl.ds(pl.multiple_of((i // 4) * 112 + first, 16), rows), pl.ds(pl.multiple_of((i % 4) * 256, 256), 256)


def both_slots(ref, i, first, rows):
    high, wide = tile(i, first, rows)
    return ref.at[:, high, wide]


def one_tile(ref, i, first, rows):
    high, wide = tile(i, first, rows)
    return ref.at[high, wide]


def result_rows(ref, i, first, rows):
    return ref.at[pl.ds(pl.multiple_of(i * 48 + first, 16), rows)]


def result_rows_in(ref, i, first, rows):
    return ref.at[pl.ds(0, 1), pl.ds(pl.multiple_of(i * 48 + first, 16), rows)]


def by_key(key, value):
    places = lax.broadcasted_iota(jnp.int32, (N, N), 0)
    return jnp.sum(jnp.where(places == key[None, :], value[None, :], 0), axis=1, dtype=jnp.int32)


def shards(base_tiles, adjusted_tiles, sketch, base_place, adjusted_place, owner_map):
    adjusted_of = by_key(base_place, adjusted_place)
    result_of = by_key(owner_map, base_place)
    chunks = ((0, 32), (32, 32), (64, 32), (96, 16))
    adjusted = route(both_slots, one_tile, 2, 256, chunks, adjusted_of, adjusted_tiles, (3584, 1024), "move_adjusted")
    result = k2(adjusted, base_tiles[0], sketch)
    moved = route(result_rows_in, result_rows, 1, 128, ((0, 48),), result_of, result[None], (6144, 128), "move_result")
    scaled_basis = moved[:3584].astype(F32) * math.sqrt(3584)
    projected = moved[3584:4608].astype(F32).reshape(8, 128, 128).transpose(1, 0, 2).reshape(128, 1024)
    return (scaled_basis[None], projected[None])


def solution(mesh):
    in_specs = (P(("grp", "ep"), None, None), P(("grp", "ep"), None, None), P(), P(), P(), P())
    out_specs = (P(("grp", "ep"), None, None), P(("grp", "ep"), None, None))
    return jax.shard_map(shards, mesh=mesh, in_specs=in_specs, out_specs=out_specs, check_vma=False)
```

time: 474 us -> 373 us (0.79)
  Pallas kernels: 470 us -> 369 us
    pallas_call x2, Pallas kernels: 390 us -> 307 us  [route(): pl.pallas_call(functools.partial(route_kernel, src_block, dst_block, slot...]
    pallas_call x1, Pallas kernels: 80.2 us -> 61.4 us  [k2(): pl.pallas_call(k2_kernel, out_shape=jax.ShapeDtypeStruct((6144, 128), BF)...]
where the time goes in v2:
time: 373 us
  Pallas kernels  369 us (99%)
    pallas_call x2, Pallas kernels, route(): pl.pallas_call(functools.partial(route_kernel, src_block, dst_block, slot...  307 us
    pallas_call x1, Pallas kernels, k2(): pl.pallas_call(k2_kernel, out_shape=jax.ShapeDtypeStruct((6144, 128), BF)...  61.4 us

profile of v2, /device:TPU:1, one launch (start us, length us, event | category | flops | bytes accessed | tf_op | source)
XLA Modules:
  0.0 373.0 jit_solution(2145687958468674539)
XLA Ops:
  0.6 0.8 select_reduce_fusion
  1.4 0.0 copy-start
  1.4 255.7 %move_adjusted.1.adj_ref = bf16[3584,1024]{1,0:T(8,128)(2,1)} custom-call(s32[128]{0:T(128)S(1)} %get-tuple-element.2.idx_ref, bf16[2,3584,1024]{2,1,0:T(8,128)(2,1)} %src_ref.1), custom_call_target="tpu_custom_call" | custom-call | tf_op jit(solution)/shard_map/move_adjusted/pallas_call | solution.py:230
  257.2 0.0 copy-done
  257.2 61.4 %factor.1 = bf16[6144,128]{1,0:T(8,128)(2,1)S(1)} custom-call(bf16[3584,1024]{1,0:T(8,128)(2,1)} %move_adjusted.1.adj_ref, bf16[3584,1024]{1,0:T(8,128)(2,1)} %bitcast.9, bf16[1024,128]{1,0:T(8,128)(2,1)S(1)} %copy-done), custom_call_target="tpu_custom_call" | custom-call | tf_op jit(solution)/shard_map/factor/pallas_call | solution.py:144
  318.6 51.7 %move_result.1 = bf16[6144,128]{1,0:T(8,128)(2,1)S(1)} custom-call(s32[128]{0:T(128)S(1)} %get-tuple-element.3.idx_ref, bf16[1,6144,128]{2,1,0:T(8,128)(2,1)S(1)} %bitcast.8), custom_call_target="tpu_custom_call" | custom-call | tf_op jit(solution)/shard_map/move_result/pallas_call | solution.py:230
  370.4 0.3 copy.9
  370.7 0.9 reshape.12
  371.6 1.4 multiply_bitcast_fusion
  (2 shorter events, 0.1 us)
Async XLA Ops:
  1.4 255.8 %copy-start = (bf16[1024,128]{1,0:T(8,128)(2,1)S(1)}, bf16[1024,128]{1,0:T(8,128)(2,1)}, u32[]{:S(2)}) copy-start(bf16[1024,128]{1,0:T(8,128)(2,1)} %s_ref.1) | copy-start | bytes 786436

commit v3 on v2

v3 whole, which is shorter than its diff:
```python
import math

import jax
import jax.numpy as jnp
from jax import lax
from jax.experimental import pallas as pl
from jax.experimental.pallas import tpu as pltpu
from jax.sharding import PartitionSpec as P

MESH = pl.DeviceIdType.MESH
N = 128
CHUNKS = ((0, 32), (32, 32), (64, 32), (96, 16))
F32 = jnp.float32
BF = jnp.bfloat16
NT = (((1,), (1,)), ((), ()))
NN = (((1,), (0,)), ((), ()))
TN = (((0,), (0,)), ((), ()))
K = 128
C = 512
NC = 7

def dot(a, b, dims):
    return lax.dot_general(a, b, dims, preferred_element_type=F32)

def split3(v):
    hi = v.astype(BF).astype(F32)
    rest = v - hi
    mid = rest.astype(BF).astype(F32)
    return hi, mid, rest - mid


def chol_inv(g_ref, w_ref):
    sub = lax.broadcasted_iota(jnp.int32, (8, K), 0)
    a = g_ref[...]
    row = lax.broadcasted_iota(jnp.int32, (K, K), 0)
    col = lax.broadcasted_iota(jnp.int32, (K, K), 1)
    x = jnp.where(row == col, 1.0, 0.0).astype(F32)
    for r0 in range(0, K, 8):
        p = a[:8]
        xp = x[:8]
        s = {}
        for i in range(8):
            for k in range(i + 1):
                s[i, k] = jnp.broadcast_to(p[i : i + 1, r0 + k : r0 + k + 1], (8, K))
        rows = [jnp.broadcast_to(p[i : i + 1, :], (8, K)) for i in range(8)]
        xrows = [jnp.broadcast_to(xp[i : i + 1, :], (8, K)) for i in range(8)]
        u = jnp.zeros((8, K), F32)
        w = jnp.zeros((8, K), F32)
        for k in range(8):
            r = lax.rsqrt(s[k, k])
            uk = rows[k] * r
            wk = xrows[k] * r
            u = jnp.where(sub == k, uk, u)
            w = jnp.where(sub == k, wk, w)
            l = {i: s[i, k] * r for i in range(k + 1, 8)}
            for i in range(k + 1, 8):
                for m in range(k + 1, i + 1):
                    s[i, m] = s[i, m] - l[i] * l[m]
            for i in range(k + 1, 8):
                rows[i] = rows[i] - l[i] * uk
                xrows[i] = xrows[i] - l[i] * wk
        w_ref[pl.ds(r0, 8), :] = w
        if r0 < K - 8:
            uh, um, ul = split3(u)
            wh, wm, wl = split3(w)
            left = jnp.concatenate([uh, uh, um, uh, ul, um], axis=0).astype(BF)
            right = jnp.concatenate(
                [
                    jnp.concatenate([uh, um, uh, ul, uh, um], axis=0).astype(BF),
                    jnp.concatenate([wh, wm, wh, wl, wh, wm], axis=0).astype(BF),
                ],
                axis=1,
            )
            upd = dot(left, right, TN)
            a = a[8:] - upd[r0 + 8 :, :K]
            x = x[8:] - upd[r0 + 8 :, K:]


def wide_left(v):
    hi = v.astype(BF)
    return jnp.concatenate([hi, hi, (v - hi.astype(F32)).astype(BF)], axis=1)


def wide_right(v):
    hi = v.astype(BF)
    return jnp.concatenate([hi, (v - hi.astype(F32)).astype(BF), hi], axis=0)


def gram(v):
    hi, mid, low = (part.astype(BF) for part in split3(v))
    first = dot(hi, jnp.concatenate([hi, mid, low], axis=0), NT)
    cross = first[:, K : 2 * K] + first[:, 2 * K :]
    return first[:, :K] + dot(mid, mid, NT) + cross + cross.T


def peer(o):
    x = lax.axis_index("grp")
    e = lax.axis_index("ep")
    o = (o * 101) % 128
    sign = 1 - 2 * (e % 2)
    tx = (x + 4 + sign * (o // 32)) % 4
    tz = (e // 8 + 4 + sign * ((o // 8) % 4)) % 4
    ty = ((e // 2) % 4 + 4 + sign * ((o // 2) % 4)) % 4
    return tx, tz * 8 + ty * 2 + (e + o) % 2


def whole(device):
    return None


def push(src, dst, send_sem, recv_sem, when=whole):
    def one(o, car):
        tx, te = peer(o)
        t = tx * 32 + te

        def start():
            pltpu.make_async_remote_copy(
                src(t), dst(t), send_sem, recv_sem, device_id=(tx, te), device_id_type=MESH
            ).start()

        if when is whole:
            start()
        else:
            pl.when(when(t))(start)
        return car

    lax.fori_loop(1, N, one, 0)


def wait_for(ref, count, sem):
    part = ref.at[pl.ds(0, count)]
    pltpu.make_async_copy(part, part, sem).wait()


def tile(i, chunk):
    first, rows = chunk
    return i // 4, pl.ds(first, rows), pl.ds(pl.multiple_of((i % 4) * 256, 256), 256)


def basis_rows(ref, i):
    return ref.at[pl.ds((i // 7) * 2, 2), pl.ds(pl.multiple_of((i % 7) * 16, 16), 16)]


def projected_rows(ref, i):
    return ref.at[pl.ds(pl.multiple_of((i // 2) * 16, 16), 16)]


def kernel(adjusted_of, result_of, adjusted, base, sketch, basis_out, projected_out, *scratch):
    parts = len(CHUNKS)
    gots = scratch[:parts]
    outs = scratch[parts : 2 * parts]
    win, d, yt, zt, g, w, basis, projected, got_q, out_q, got_p, out_p = scratch[2 * parts : 2 * parts + 12]
    ssem, rsem, s2sem, r2sem, lsem, l2sem, base_sem, qsem, psem = scratch[2 * parts + 12 :]
    me = lax.axis_index("grp") * 32 + lax.axis_index("ep")
    mine = pl.ds(2 * me, 2)

    base_copy = pltpu.make_async_copy(base.at[0], d, base_sem)
    base_copy.start()

    def stored(i, k):
        block, high, wide = tile(i, CHUNKS[k])
        return adjusted.at[:, block, high, wide]

    def landed(k):
        block, high, wide = tile(me, CHUNKS[k])
        return win.at[block, high, wide]

    def own(k):
        return pltpu.make_async_copy(stored(me, k), gots[k].at[mine], lsem.at[k])

    def own2(k):
        return pltpu.make_async_copy(outs[k].at[me], landed(k), l2sem.at[k])

    for k in range(parts):
        own(k).start()
        push(lambda t, k=k: stored(t, k), lambda t, k=k: gots[k].at[mine], ssem.at[k], rsem.at[k])
    st = sketch[...].astype(F32).T.astype(BF)
    for k in range(parts):
        own(k).wait()
        wait_for(gots[k], 2 * (N - 1), rsem.at[k])

        def pick(b, car, k=k):
            outs[k][b] = gots[k][adjusted_of[b]]
            return car

        lax.fori_loop(0, N, pick, 0)
        own2(k).start()
        push(lambda t, k=k: outs[k].at[t], lambda t, k=k: landed(k), s2sem.at[k], r2sem.at[k])

    base_copy.wait()
    g[...] = jnp.zeros_like(g)

    def rows_of(c):
        return pl.ds(pl.multiple_of(c * 16, 16), 16)

    def delta(c):
        return d[:, rows_of(c), :].reshape(C, 1024)

    def first(c, car):
        apart = win[:, rows_of(c), :].reshape(C, 1024).astype(F32) - delta(c).astype(F32)
        dc = apart.astype(BF)
        d[:, rows_of(c), :] = dc.reshape(32, 16, 1024)
        y = dot(st, dc, NT)
        yt[c] = y
        g[...] += gram(y)
        return car

    for k in range(parts):
        own2(k).wait()
        wait_for(outs[k], N - 1, r2sem.at[k])
        low, rows = CHUNKS[k]
        lax.fori_loop(low // 16, (low + rows) // 16, first, 0)

    def project():
        def body(c, car):
            q = dot(wide_left(w[...]), wide_right(yt[c]), NN)
            zt[...] += dot(q.astype(BF), delta(c), NN)
            return car

        zt[...] = jnp.zeros_like(zt)
        lax.fori_loop(0, NC, body, 0)

    def step(t, car):
        chol_inv(g, w)

        @pl.when(t % 2 == 0)
        def _():
            project()
            g[...] = gram(zt[...])

        @pl.when(t % 2 == 1)
        def _():
            at = dot(wide_left(w[...]), wide_right(zt[...]), NN).astype(BF)
            g[...] = jnp.zeros_like(g)

            def back(c, car):
                y = dot(at, delta(c), NT)
                yt[c] = y
                g[...] += gram(y)
                return car

            lax.fori_loop(0, NC, back, 0)

        return car

    lax.fori_loop(0, 4, step, 0)
    chol_inv(g, w)

    def last(c, car):
        q = dot(wide_left(w[...]), wide_right(yt[c]), NN)
        basis[:, rows_of(c), :] = q.T.astype(BF).reshape(32, 16, K)
        yt[c] = q
        return car

    lax.fori_loop(0, NC, last, 0)
    relay = me < 112
    even = me % 2 == 0

    def both(condition, yes, no):
        pl.when(condition)(yes)
        pl.when(jnp.logical_not(condition))(no)

    own_q = pltpu.make_async_copy(basis_rows(basis, me), got_q.at[me], qsem.at[4])
    own_q2 = pltpu.make_async_copy(out_q.at[me], basis_rows(basis_out, me), qsem.at[5])
    own_p = pltpu.make_async_copy(projected_rows(projected, me), got_p.at[me], psem.at[4])
    own_p2 = pltpu.make_async_copy(out_p.at[me], projected_rows(projected_out, me), psem.at[5])

    push(lambda t: basis_rows(basis, t), lambda t: got_q.at[me], qsem.at[0], qsem.at[1], lambda t: t < 112)
    pl.when(relay)(own_q.start)

    zt[...] = jnp.zeros_like(zt)

    def final(c, car):
        zt[...] += dot(yt[c].astype(BF), delta(c), NN)
        return car

    lax.fori_loop(0, NC, final, 0)
    for j in range(8):
        projected[K * j : K * (j + 1), :] = zt[:, K * j : K * (j + 1)].astype(BF)
    push(lambda t: projected_rows(projected, t), lambda t: got_p.at[me], psem.at[0], psem.at[1], lambda t: t % 2 == 0)
    pl.when(even)(own_p.start)

    @pl.when(relay)
    def _():
        own_q.wait()
        wait_for(got_q, N - 1, qsem.at[1])

        def pick(b, car):
            out_q[b] = got_q[result_of[b]]
            return car

        lax.fori_loop(0, N, pick, 0)
        own_q2.start()
        push(lambda t: out_q.at[t], lambda t: basis_rows(basis_out, me), qsem.at[2], qsem.at[3])

    @pl.when(even)
    def _():
        own_p.wait()
        wait_for(got_p, N - 1, psem.at[1])

        def pick(b, car):
            out_p[b] = got_p[result_of[b]]
            return car

        lax.fori_loop(0, N, pick, 0)
        own_p2.start()
        push(lambda t: out_p.at[t], lambda t: projected_rows(projected_out, me), psem.at[2], psem.at[3])

    for k in range(parts):
        wait_for(gots[k], 2 * (N - 1), ssem.at[k])
        wait_for(outs[k], N - 1, s2sem.at[k])

    @pl.when(relay)
    def _():
        own_q2.wait()
        wait_for(out_q, 111, qsem.at[0])
        wait_for(out_q, 111, qsem.at[3])
        wait_for(out_q, N - 1, qsem.at[2])

    @pl.when(jnp.logical_not(relay))
    def _():
        wait_for(out_q, 112, qsem.at[0])
        wait_for(out_q, 112, qsem.at[3])

    @pl.when(even)
    def _():
        own_p2.wait()
        wait_for(out_p, 63, psem.at[0])
        wait_for(out_p, 63, psem.at[3])
        wait_for(out_p, N - 1, psem.at[2])

    @pl.when(jnp.logical_not(even))
    def _():
        wait_for(out_p, 64, psem.at[0])
        wait_for(out_p, 64, psem.at[3])


def relocate_and_factor(adjusted_of, result_of, adjusted, base, sketch):
    smem = pl.BlockSpec(memory_space=pltpu.SMEM)
    anywhere = pl.BlockSpec(memory_space=pl.ANY)
    parts = len(CHUNKS)
    return pl.pallas_call(
        kernel,
        out_shape=(jax.ShapeDtypeStruct((32, 112, K), BF), jax.ShapeDtypeStruct((1024, K), BF)),
        in_specs=[smem, smem, anywhere, anywhere, pl.BlockSpec(memory_space=pltpu.VMEM)],
        out_specs=(anywhere, anywhere),
        scratch_shapes=[pltpu.VMEM((2 * N, rows, 256), BF) for _, rows in CHUNKS]
        + [pltpu.VMEM((N, rows, 256), BF) for _, rows in CHUNKS]
        + [
            pltpu.VMEM((32, 112, 1024), BF),
            pltpu.VMEM((32, 112, 1024), BF),
            pltpu.VMEM((NC, K, C), F32),
            pltpu.VMEM((K, 1024), F32),
            pltpu.VMEM((K, K), F32),
            pltpu.VMEM((K, K), F32),
            pltpu.VMEM((32, 112, K), BF),
            pltpu.VMEM((1024, K), BF),
            pltpu.VMEM((N, 2, 16, K), BF),
            pltpu.VMEM((N, 2, 16, K), BF),
            pltpu.VMEM((N, 16, K), BF),
            pltpu.VMEM((N, 16, K), BF),
        ]
        + [pltpu.SemaphoreType.DMA((parts,))] * 6
        + [pltpu.SemaphoreType.DMA, pltpu.SemaphoreType.DMA((6,)), pltpu.SemaphoreType.DMA((6,))],
        compiler_params=pltpu.CompilerParams(has_side_effects=True, vmem_limit_bytes=54 * 2**20),
        name="relocate_and_factor",
    )(adjusted_of, result_of, adjusted.reshape(2, 32, 112, 1024), base.reshape(1, 32, 112, 1024), sketch)


def by_key(key, value):
    places = lax.broadcasted_iota(jnp.int32, (N, N), 0)
    return jnp.sum(jnp.where(places == key[None, :], value[None, :], 0), axis=1, dtype=jnp.int32)


def shards(base_tiles, adjusted_tiles, sketch, base_place, adjusted_place, owner_map):
    adjusted_of = by_key(base_place, adjusted_place)
    result_of = by_key(owner_map, base_place)
    basis, projected = relocate_and_factor(adjusted_of, result_of, adjusted_tiles, base_tiles, sketch)
    scaled_basis = basis.reshape(3584, K).astype(F32) * math.sqrt(3584)
    projected = projected.astype(F32).reshape(8, K, K).transpose(1, 0, 2).reshape(K, 1024)
    return (scaled_basis[None], projected[None])


def solution(mesh):
    in_specs = (P(("grp", "ep"), None, None), P(("grp", "ep"), None, None), P(), P(), P(), P())
    out_specs = (P(("grp", "ep"), None, None), P(("grp", "ep"), None, None))
    return jax.shard_map(shards, mesh=mesh, in_specs=in_specs, out_specs=out_specs, check_vma=False)
```

time: 373 us -> 351 us (0.941)
  Pallas kernels: 369 us -> 345 us
    pallas_call x3 -> x1, Pallas kernels: 369 us -> 345 us  [relocate_and_factor(): pl.pallas_call(kernel, out_shape=(jax.ShapeDtypeStruct((32, 112, K), BF),...]
where the time goes in v3:
time: 351 us; the launch traced here: 350 us
  Pallas kernels  345 us (98%)
  other arithmetic  3.94 us (1%)
    pallas_call x1, Pallas kernels, relocate_and_factor(): pl.pallas_call(kernel, out_shape=(jax.ShapeDtypeStruct((32, 112, K), BF),...  345 us

profile of v3, /device:TPU:1, one launch (start us, length us, event | category | flops | bytes accessed | tf_op | source)
XLA Modules:
  0.0 350.4 jit_solution(6691119238663634638)
XLA Ops:
  0.6 1.3 select_reduce_fusion
  1.9 344.6 %relocate_and_factor.1 = (bf16[32,112,128]{2,1,0:T(8,128)(2,1)}, bf16[1024,128]{1,0:T(8,128)(2,1)}) custom-call(s32[128]{0:T(128)} %get-tuple-element.7.adjusted_of, s32[128]{0:T(128)} %get-tuple-element.6.result_of, bf16[2,32,112,1024]{3,2,1,0:T(8,128)(2,1)} %bitcast.7, bf16[1,32,112,1024]{3,2,1,0:T(8,128)(2,1)} %bitcast.8, bf16[1024,128]{1,0:T(8,128)(2,1)} %sketch.1), custom_call_target="tpu_custom_call" | custom-call | tf_op jit(solution)/shard_map/relocate_and_factor/pallas_call | solution.py:342
  346.6 0.0 copy-start
  346.6 2.6 convert_multiply_fusion
  349.2 0.0 copy-done
  349.2 0.3 copy.9
  349.5 0.9 reshape.37
  (1 shorter events, 0.0 us)
Async XLA Ops:
  346.6 2.6 copy-start

commit v4 on v3

--- a/solution.py
+++ b/solution.py
@@ -16,8 +16,10 @@
 NN = (((1,), (0,)), ((), ()))
 TN = (((0,), (0,)), ((), ()))
 K = 128
+BLOCK = 32
 C = 512
-NC = 7
+ROWS = 3584
+HALF = ROWS // 2
 
 def dot(a, b, dims):
     return lax.dot_general(a, b, dims, preferred_element_type=F32)
@@ -35,34 +37,48 @@
     row = lax.broadcasted_iota(jnp.int32, (K, K), 0)
     col = lax.broadcasted_iota(jnp.int32, (K, K), 1)
     x = jnp.where(row == col, 1.0, 0.0).astype(F32)
-    for r0 in range(0, K, 8):
-        p = a[:8]
-        xp = x[:8]
-        s = {}
-        for i in range(8):
-            for k in range(i + 1):
-                s[i, k] = jnp.broadcast_to(p[i : i + 1, r0 + k : r0 + k + 1], (8, K))
-        rows = [jnp.broadcast_to(p[i : i + 1, :], (8, K)) for i in range(8)]
-        xrows = [jnp.broadcast_to(xp[i : i + 1, :], (8, K)) for i in range(8)]
-        u = jnp.zeros((8, K), F32)
-        w = jnp.zeros((8, K), F32)
-        for k in range(8):
-            r = lax.rsqrt(s[k, k])
-            uk = rows[k] * r
-            wk = xrows[k] * r
-            u = jnp.where(sub == k, uk, u)
-            w = jnp.where(sub == k, wk, w)
-            l = {i: s[i, k] * r for i in range(k + 1, 8)}
-            for i in range(k + 1, 8):
-                for m in range(k + 1, i + 1):
-                    s[i, m] = s[i, m] - l[i] * l[m]
-            for i in range(k + 1, 8):
-                rows[i] = rows[i] - l[i] * uk
-                xrows[i] = xrows[i] - l[i] * wk
-        w_ref[pl.ds(r0, 8), :] = w
-        if r0 < K - 8:
-            uh, um, ul = split3(u)
-            wh, wm, wl = split3(w)
+    for b0 in range(0, K, BLOCK):
+        panel = [a[i : i + 8] for i in range(0, BLOCK, 8)]
+        side = [x[i : i + 8] for i in range(0, BLOCK, 8)]
+        us = []
+        ws = []
+        for r0 in range(b0, b0 + BLOCK, 8):
+            p = panel.pop(0)
+            xp = side.pop(0)
+            s = {}
+            for i in range(8):
+                for k in range(i + 1):
+                    s[i, k] = jnp.broadcast_to(p[i : i + 1, r0 + k : r0 + k + 1], (8, K))
+            rows = [jnp.broadcast_to(p[i : i + 1, :], (8, K)) for i in range(8)]
+            xrows = [jnp.broadcast_to(xp[i : i + 1, :], (8, K)) for i in range(8)]
+            below = [[jnp.broadcast_to(q[:, r0 + k : r0 + k + 1], (8, K)) for k in range(8)] for q in panel]
+            u = jnp.zeros((8, K), F32)
+            w = jnp.zeros((8, K), F32)
+            for k in range(8):
+                r = lax.rsqrt(s[k, k])
+                uk = rows[k] * r
+                wk = xrows[k] * r
+                u = jnp.where(sub == k, uk, u)
+                w = jnp.where(sub == k, wk, w)
+                l = {i: s[i, k] * r for i in range(k + 1, 8)}
+                for i in range(k + 1, 8):
+                    for m in range(k + 1, i + 1):
+                        s[i, m] = s[i, m] - l[i] * l[m]
+                for i in range(k + 1, 8):
+                    rows[i] = rows[i] - l[i] * uk
+                    xrows[i] = xrows[i] - l[i] * wk
+                for n, c in enumerate(below):
+                    ck = c[k] * r
+                    for m in range(k + 1, 8):
+                        c[m] = c[m] - ck * l[m]
+                    panel[n] = panel[n] - ck * uk
+                    side[n] = side[n] - ck * wk
+            w_ref[pl.ds(r0, 8), :] = w
+            us.append(u)
+            ws.append(w)
+        if b0 < K - BLOCK:
+            uh, um, ul = split3(jnp.concatenate(us, axis=0))
+            wh, wm, wl = split3(jnp.concatenate(ws, axis=0))
             left = jnp.concatenate([uh, uh, um, uh, ul, um], axis=0).astype(BF)
             right = jnp.concatenate(
                 [
@@ -72,8 +88,8 @@
                 axis=1,
             )
             upd = dot(left, right, TN)
-            a = a[8:] - upd[r0 + 8 :, :K]
-            x = x[8:] - upd[r0 + 8 :, K:]
+            a = a[BLOCK:] - upd[b0 + BLOCK :, :K]
+            x = x[BLOCK:] - upd[b0 + BLOCK :, K:]
 
 
 def wide_left(v):
@@ -138,7 +154,7 @@
 
 
 def basis_rows(ref, i):
-    return ref.at[pl.ds((i // 7) * 2, 2), pl.ds(pl.multiple_of((i % 7) * 16, 16), 16)]
+    return ref.at[pl.ds((i % 16) * 2, 2), pl.ds(pl.multiple_of((i // 16) * 16, 16), 16)]
 
 
 def projected_rows(ref, i):
@@ -149,12 +165,12 @@
     parts = len(CHUNKS)
     gots = scratch[:parts]
     outs = scratch[parts : 2 * parts]
-    win, d, yt, zt, g, w, basis, projected, got_q, out_q, got_p, out_p = scratch[2 * parts : 2 * parts + 12]
-    ssem, rsem, s2sem, r2sem, lsem, l2sem, base_sem, qsem, psem = scratch[2 * parts + 12 :]
+    win, old, d, yt, zt, g, w, basis, projected, got_q, out_q, got_p, out_p = scratch[2 * parts : 2 * parts + 13]
+    ssem, rsem, s2sem, r2sem, lsem, l2sem, base_sem, qsem, psem = scratch[2 * parts + 13 :]
     me = lax.axis_index("grp") * 32 + lax.axis_index("ep")
     mine = pl.ds(2 * me, 2)
 
-    base_copy = pltpu.make_async_copy(base.at[0], d, base_sem)
+    base_copy = pltpu.make_async_copy(base.at[0], old, base_sem)
     base_copy.start()
 
     def stored(i, k):
@@ -190,18 +206,14 @@
     base_copy.wait()
     g[...] = jnp.zeros_like(g)
 
-    def rows_of(c):
-        return pl.ds(pl.multiple_of(c * 16, 16), 16)
-
-    def delta(c):
-        return d[:, rows_of(c), :].reshape(C, 1024)
-
     def first(c, car):
-        apart = win[:, rows_of(c), :].reshape(C, 1024).astype(F32) - delta(c).astype(F32)
+        rows = pl.ds(pl.multiple_of(c * 16, 16), 16)
+        apart = win[:, rows, :].reshape(C, 1024).astype(F32) - old[:, rows, :].reshape(C, 1024).astype(F32)
         dc = apart.astype(BF)
-        d[:, rows_of(c), :] = dc.reshape(32, 16, 1024)
+        here = pl.ds(pl.multiple_of(c * C, C), C)
+        d[here, :] = dc
         y = dot(st, dc, NT)
-        yt[c] = y
+        yt[:, here] = y
         g[...] += gram(y)
         return car
 
@@ -211,48 +223,41 @@
         low, rows = CHUNKS[k]
         lax.fori_loop(low // 16, (low + rows) // 16, first, 0)
 
-    def project():
-        def body(c, car):
-            q = dot(wide_left(w[...]), wide_right(yt[c]), NN)
-            zt[...] += dot(q.astype(BF), delta(c), NN)
-            return car
-
-        zt[...] = jnp.zeros_like(zt)
-        lax.fori_loop(0, NC, body, 0)
+    halves = (pl.ds(0, HALF), pl.ds(HALF, HALF))
 
     def step(t, car):
         chol_inv(g, w)
+        left = wide_left(w[...])
 
         @pl.when(t % 2 == 0)
         def _():
-            project()
-            g[...] = gram(zt[...])
+            total = jnp.zeros((K, 1024), F32)
+            for h in halves:
+                q = dot(left, wide_right(yt[:, h]), NN)
+                total = total + dot(q.astype(BF), d[h, :], NN)
+            zt[...] = total
+            g[...] = gram(total)
 
         @pl.when(t % 2 == 1)
         def _():
-            at = dot(wide_left(w[...]), wide_right(zt[...]), NN).astype(BF)
-            g[...] = jnp.zeros_like(g)
-
-            def back(c, car):
-                y = dot(at, delta(c), NT)
-                yt[c] = y
-                g[...] += gram(y)
-                return car
-
-            lax.fori_loop(0, NC, back, 0)
+            across = dot(left, wide_right(zt[...]), NN).astype(BF)
+            total = jnp.zeros((K, K), F32)
+            for h in halves:
+                y = dot(across, d[h, :], NT)
+                yt[:, h] = y
+                total = total + gram(y)
+            g[...] = total
 
         return car
 
     lax.fori_loop(0, 4, step, 0)
     chol_inv(g, w)
 
-    def last(c, car):
-        q = dot(wide_left(w[...]), wide_right(yt[c]), NN)
-        basis[:, rows_of(c), :] = q.T.astype(BF).reshape(32, 16, K)
-        yt[c] = q
-        return car
-
-    lax.fori_loop(0, NC, last, 0)
+    left = wide_left(w[...])
+    for n, h in enumerate(halves):
+        q = dot(left, wide_right(yt[:, h]), NN)
+        basis[56 * n : 56 * (n + 1)] = q.T.astype(BF).reshape(56, 2, 16, K)
+        yt[:, h] = q
     relay = me < 112
     even = me % 2 == 0
 
@@ -260,23 +265,19 @@
         pl.when(condition)(yes)
         pl.when(jnp.logical_not(condition))(no)
 
-    own_q = pltpu.make_async_copy(basis_rows(basis, me), got_q.at[me], qsem.at[4])
+    own_q = pltpu.make_async_copy(basis.at[me % 112], got_q.at[me], qsem.at[4])
     own_q2 = pltpu.make_async_copy(out_q.at[me], basis_rows(basis_out, me), qsem.at[5])
     own_p = pltpu.make_async_copy(projected_rows(projected, me), got_p.at[me], psem.at[4])
     own_p2 = pltpu.make_async_copy(out_p.at[me], projected_rows(projected_out, me), psem.at[5])
 
-    push(lambda t: basis_rows(basis, t), lambda t: got_q.at[me], qsem.at[0], qsem.at[1], lambda t: t < 112)
+    push(lambda t: basis.at[t], lambda t: got_q.at[me], qsem.at[0], qsem.at[1], lambda t: t < 112)
     pl.when(relay)(own_q.start)
 
-    zt[...] = jnp.zeros_like(zt)
-
-    def final(c, car):
-        zt[...] += dot(yt[c].astype(BF), delta(c), NN)
-        return car
-
-    lax.fori_loop(0, NC, final, 0)
+    total = jnp.zeros((K, 1024), F32)
+    for h in halves:
+        total = total + dot(yt[:, h].astype(BF), d[h, :], NN)
     for j in range(8):
-        projected[K * j : K * (j + 1), :] = zt[:, K * j : K * (j + 1)].astype(BF)
+        projected[K * j : K * (j + 1), :] = total[:, K * j : K * (j + 1)].astype(BF)
     push(lambda t: projected_rows(projected, t), lambda t: got_p.at[me], psem.at[0], psem.at[1], lambda t: t % 2 == 0)
     pl.when(even)(own_p.start)
 
@@ -349,11 +350,12 @@
         + [
             pltpu.VMEM((32, 112, 1024), BF),
             pltpu.VMEM((32, 112, 1024), BF),
-            pltpu.VMEM((NC, K, C), F32),
+            pltpu.VMEM((ROWS, 1024), BF),
+            pltpu.VMEM((K, ROWS), F32),
             pltpu.VMEM((K, 1024), F32),
             pltpu.VMEM((K, K), F32),
             pltpu.VMEM((K, K), F32),
-            pltpu.VMEM((32, 112, K), BF),
+            pltpu.VMEM((112, 2, 16, K), BF),
             pltpu.VMEM((1024, K), BF),
             pltpu.VMEM((N, 2, 16, K), BF),
             pltpu.VMEM((N, 2, 16, K), BF),
@@ -362,7 +364,7 @@
         ]
         + [pltpu.SemaphoreType.DMA((parts,))] * 6
         + [pltpu.SemaphoreType.DMA, pltpu.SemaphoreType.DMA((6,)), pltpu.SemaphoreType.DMA((6,))],
-        compiler_params=pltpu.CompilerParams(has_side_effects=True, vmem_limit_bytes=54 * 2**20),
+        compiler_params=pltpu.CompilerParams(has_side_effects=True, vmem_limit_bytes=58 * 2**20),
         name="relocate_and_factor",
     )(adjusted_of, result_of, adjusted.reshape(2, 32, 112, 1024), base.reshape(1, 32, 112, 1024), sketch)
 
@@ -376,7 +378,7 @@
     adjusted_of = by_key(base_place, adjusted_place)
     result_of = by_key(owner_map, base_place)
     basis, projected = relocate_and_factor(adjusted_of, result_of, adjusted_tiles, base_tiles, sketch)
-    scaled_basis = basis.reshape(3584, K).astype(F32) * math.sqrt(3584)
+    scaled_basis = basis.reshape(ROWS, K).astype(F32) * math.sqrt(ROWS)
     projected = projected.astype(F32).reshape(8, K, K).transpose(1, 0, 2).reshape(K, 1024)
     return (scaled_basis[None], projected[None])
 

time: 351 us -> 331 us (0.943)
  Pallas kernels: 345 us -> 325 us
    pallas_call x1, Pallas kernels: 345 us -> 325 us  [relocate_and_factor(): pl.pallas_call(kernel, out_shape=(jax.ShapeDtypeStruct((32, 112, K), BF),...]
where the time goes in v4:
time: 331 us; the launch traced here: 330 us
  Pallas kernels  325 us (98%)
  other arithmetic  3.94 us (1%)
    pallas_call x1, Pallas kernels, relocate_and_factor(): pl.pallas_call(kernel, out_shape=(jax.ShapeDtypeStruct((32, 112, K), BF),...  325 us

profile of v4, /device:TPU:1, one launch (start us, length us, event | category | flops | bytes accessed | tf_op | source)
XLA Modules:
  0.0 330.4 jit_solution(17150973607892319511)
XLA Ops:
  0.6 1.3 select_reduce_fusion
  1.9 324.6 %relocate_and_factor.1 = (bf16[32,112,128]{2,1,0:T(8,128)(2,1)}, bf16[1024,128]{1,0:T(8,128)(2,1)}) custom-call(s32[128]{0:T(128)} %get-tuple-element.7.adjusted_of, s32[128]{0:T(128)} %get-tuple-element.6.result_of, bf16[2,32,112,1024]{3,2,1,0:T(8,128)(2,1)} %bitcast.7, bf16[1,32,112,1024]{3,2,1,0:T(8,128)(2,1)} %bitcast.8, bf16[1024,128]{1,0:T(8,128)(2,1)} %sketch.1), custom_call_target="tpu_custom_call" | custom-call | tf_op jit(solution)/shard_map/relocate_and_factor/pallas_call | solution.py:343
  326.6 0.0 copy-start
  326.6 2.6 convert_multiply_fusion
  329.2 0.0 copy-done
  329.2 0.3 copy.9
  329.5 0.9 reshape.37
  (1 shorter events, 0.0 us)
Async XLA Ops:
  326.6 2.6 copy-start

commit v5 on v4

--- a/solution.py
+++ b/solution.py
@@ -31,7 +31,7 @@
     return hi, mid, rest - mid
 
 
-def chol_inv(g_ref, w_ref):
+def chol_inv(g_ref, w_ref, t_ref):
     sub = lax.broadcasted_iota(jnp.int32, (8, K), 0)
     a = g_ref[...]
     row = lax.broadcasted_iota(jnp.int32, (K, K), 0)
@@ -46,11 +46,16 @@
             p = panel.pop(0)
             xp = side.pop(0)
             s = {}
+            held = t_ref.at[r0 // 8 % 2]
+            for k in range(8):
+                held[k] = jnp.broadcast_to(p[:, r0 + k : r0 + k + 1], (8, K))
+            held[8] = p
+            held[9] = xp
             for i in range(8):
                 for k in range(i + 1):
-                    s[i, k] = jnp.broadcast_to(p[i : i + 1, r0 + k : r0 + k + 1], (8, K))
-            rows = [jnp.broadcast_to(p[i : i + 1, :], (8, K)) for i in range(8)]
-            xrows = [jnp.broadcast_to(xp[i : i + 1, :], (8, K)) for i in range(8)]
+                    s[i, k] = jnp.broadcast_to(held[k, i : i + 1, :], (8, K))
+            rows = [jnp.broadcast_to(held[8, i : i + 1, :], (8, K)) for i in range(8)]
+            xrows = [jnp.broadcast_to(held[9, i : i + 1, :], (8, K)) for i in range(8)]
             below = [[jnp.broadcast_to(q[:, r0 + k : r0 + k + 1], (8, K)) for k in range(8)] for q in panel]
             u = jnp.zeros((8, K), F32)
             w = jnp.zeros((8, K), F32)
@@ -112,12 +117,12 @@
 def peer(o):
     x = lax.axis_index("grp")
     e = lax.axis_index("ep")
-    o = (o * 101) % 128
-    sign = 1 - 2 * (e % 2)
-    tx = (x + 4 + sign * (o // 32)) % 4
-    tz = (e // 8 + 4 + sign * ((o // 8) % 4)) % 4
-    ty = ((e // 2) % 4 + 4 + sign * ((o // 2) % 4)) % 4
-    return tx, tz * 8 + ty * 2 + (e + o) % 2
+    o = lax.rem(o * 101, 128)
+    sign = 1 - 2 * lax.rem(e, 2)
+    tx = lax.rem(x + 4 + sign * lax.div(o, 32), 4)
+    tz = lax.rem(lax.div(e, 8) + 4 + sign * lax.rem(lax.div(o, 8), 4), 4)
+    ty = lax.rem(lax.rem(lax.div(e, 2), 4) + 4 + sign * lax.rem(lax.div(o, 2), 4), 4)
+    return tx, tz * 8 + ty * 2 + lax.rem(e + o, 2)
 
 
 def whole(device):
@@ -140,7 +145,7 @@
             pl.when(when(t))(start)
         return car
 
-    lax.fori_loop(1, N, one, 0)
+    lax.fori_loop(1, N, one, 0, unroll=3)
 
 
 def wait_for(ref, count, sem):
@@ -153,8 +158,12 @@
     return i // 4, pl.ds(first, rows), pl.ds(pl.multiple_of((i % 4) * 256, 256), 256)
 
 
-def basis_rows(ref, i):
-    return ref.at[pl.ds((i % 16) * 2, 2), pl.ds(pl.multiple_of((i // 16) * 16, 16), 16)]
+def entry(i):
+    return lax.rem(i * 37, N)
+
+
+def basis_rows(ref, n):
+    return ref.at[pl.ds(lax.rem(n, 16) * 2, 2), pl.ds(pl.multiple_of(lax.div(n, 16) * 16, 16), 16)]
 
 
 def projected_rows(ref, i):
@@ -165,8 +174,8 @@
     parts = len(CHUNKS)
     gots = scratch[:parts]
     outs = scratch[parts : 2 * parts]
-    win, old, d, yt, zt, g, w, basis, projected, got_q, out_q, got_p, out_p = scratch[2 * parts : 2 * parts + 13]
-    ssem, rsem, s2sem, r2sem, lsem, l2sem, base_sem, qsem, psem = scratch[2 * parts + 13 :]
+    win, old, d, yt, zt, g, w, spread, basis, projected, got_q, out_q, got_p, out_p = scratch[2 * parts : 2 * parts + 14]
+    ssem, rsem, s2sem, r2sem, lsem, l2sem, base_sem, qsem, psem = scratch[2 * parts + 14 :]
     me = lax.axis_index("grp") * 32 + lax.axis_index("ep")
     mine = pl.ds(2 * me, 2)
 
@@ -199,7 +208,7 @@
             outs[k][b] = gots[k][adjusted_of[b]]
             return car
 
-        lax.fori_loop(0, N, pick, 0)
+        lax.fori_loop(0, N, pick, 0, unroll=4)
         own2(k).start()
         push(lambda t, k=k: outs[k].at[t], lambda t, k=k: landed(k), s2sem.at[k], r2sem.at[k])
 
@@ -226,7 +235,7 @@
     halves = (pl.ds(0, HALF), pl.ds(HALF, HALF))
 
     def step(t, car):
-        chol_inv(g, w)
+        chol_inv(g, w, spread)
         left = wide_left(w[...])
 
         @pl.when(t % 2 == 0)
@@ -251,26 +260,27 @@
         return car
 
     lax.fori_loop(0, 4, step, 0)
-    chol_inv(g, w)
+    chol_inv(g, w, spread)
 
     left = wide_left(w[...])
     for n, h in enumerate(halves):
         q = dot(left, wide_right(yt[:, h]), NN)
         basis[56 * n : 56 * (n + 1)] = q.T.astype(BF).reshape(56, 2, 16, K)
         yt[:, h] = q
-    relay = me < 112
+    place = entry(me)
+    relay = place < 112
     even = me % 2 == 0
 
     def both(condition, yes, no):
         pl.when(condition)(yes)
         pl.when(jnp.logical_not(condition))(no)
 
-    own_q = pltpu.make_async_copy(basis.at[me % 112], got_q.at[me], qsem.at[4])
-    own_q2 = pltpu.make_async_copy(out_q.at[me], basis_rows(basis_out, me), qsem.at[5])
+    own_q = pltpu.make_async_copy(basis.at[lax.rem(place, 112)], got_q.at[me], qsem.at[4])
+    own_q2 = pltpu.make_async_copy(out_q.at[me], basis_rows(basis_out, place), qsem.at[5])
     own_p = pltpu.make_async_copy(projected_rows(projected, me), got_p.at[me], psem.at[4])
     own_p2 = pltpu.make_async_copy(out_p.at[me], projected_rows(projected_out, me), psem.at[5])
 
-    push(lambda t: basis.at[t], lambda t: got_q.at[me], qsem.at[0], qsem.at[1], lambda t: t < 112)
+    push(lambda t: basis.at[entry(t)], lambda t: got_q.at[me], qsem.at[0], qsem.at[1], lambda t: entry(t) < 112)
     pl.when(relay)(own_q.start)
 
     total = jnp.zeros((K, 1024), F32)
@@ -290,9 +300,9 @@
             out_q[b] = got_q[result_of[b]]
             return car
 
-        lax.fori_loop(0, N, pick, 0)
+        lax.fori_loop(0, N, pick, 0, unroll=4)
         own_q2.start()
-        push(lambda t: out_q.at[t], lambda t: basis_rows(basis_out, me), qsem.at[2], qsem.at[3])
+        push(lambda t: out_q.at[t], lambda t: basis_rows(basis_out, place), qsem.at[2], qsem.at[3])
 
     @pl.when(even)
     def _():
@@ -303,7 +313,7 @@
             out_p[b] = got_p[result_of[b]]
             return car
 
-        lax.fori_loop(0, N, pick, 0)
+        lax.fori_loop(0, N, pick, 0, unroll=4)
         own_p2.start()
         push(lambda t: out_p.at[t], lambda t: projected_rows(projected_out, me), psem.at[2], psem.at[3])
 
@@ -355,6 +365,7 @@
             pltpu.VMEM((K, 1024), F32),
             pltpu.VMEM((K, K), F32),
             pltpu.VMEM((K, K), F32),
+            pltpu.VMEM((2, 10, 8, K), F32),
             pltpu.VMEM((112, 2, 16, K), BF),
             pltpu.VMEM((1024, K), BF),
             pltpu.VMEM((N, 2, 16, K), BF),

time: 331 us -> 327 us (0.988)
  Pallas kernels: 325 us -> 321 us
    pallas_call x1, Pallas kernels: 325 us -> 321 us  [relocate_and_factor(): pl.pallas_call(kernel, out_shape=(jax.ShapeDtypeStruct((32, 112, K), BF),...]
where the time goes in v5:
time: 327 us
  Pallas kernels  321 us (98%)
  other arithmetic  3.94 us (1%)
    pallas_call x1, Pallas kernels, relocate_and_factor(): pl.pallas_call(kernel, out_shape=(jax.ShapeDtypeStruct((32, 112, K), BF),...  321 us

profile of v5, /device:TPU:1, one launch (start us, length us, event | category | flops | bytes accessed | tf_op | source)
XLA Modules:
  0.0 326.6 jit_solution(10594650316185181858)
XLA Ops:
  0.6 1.3 select_reduce_fusion
  1.9 320.8 %relocate_and_factor.1 = (bf16[32,112,128]{2,1,0:T(8,128)(2,1)}, bf16[1024,128]{1,0:T(8,128)(2,1)}) custom-call(s32[128]{0:T(128)} %get-tuple-element.7.adjusted_of, s32[128]{0:T(128)} %get-tuple-element.6.result_of, bf16[2,32,112,1024]{3,2,1,0:T(8,128)(2,1)} %bitcast.7, bf16[1,32,112,1024]{3,2,1,0:T(8,128)(2,1)} %bitcast.8, bf16[1024,128]{1,0:T(8,128)(2,1)} %sketch.1), custom_call_target="tpu_custom_call" | custom-call | tf_op jit(solution)/shard_map/relocate_and_factor/pallas_call | solution.py:353
  322.8 0.0 copy-start
  322.8 2.6 convert_multiply_fusion
  325.4 0.0 copy-done
  325.4 0.3 copy.9
  325.7 0.9 reshape.37
  (1 shorter events, 0.0 us)
Async XLA Ops:
  322.8 2.6 copy-start

commit v6 on v5

--- a/solution.py
+++ b/solution.py
@@ -174,13 +174,16 @@
     parts = len(CHUNKS)
     gots = scratch[:parts]
     outs = scratch[parts : 2 * parts]
-    win, old, d, yt, zt, g, w, spread, basis, projected, got_q, out_q, got_p, out_p = scratch[2 * parts : 2 * parts + 14]
-    ssem, rsem, s2sem, r2sem, lsem, l2sem, base_sem, qsem, psem = scratch[2 * parts + 14 :]
+    win, d, yt, zt, g, w, spread, basis, projected, got_q, out_q, got_p, out_p = scratch[2 * parts : 2 * parts + 13]
+    ssem, rsem, s2sem, r2sem, lsem, l2sem, base_sem, qsem, psem = scratch[2 * parts + 13 :]
     me = lax.axis_index("grp") * 32 + lax.axis_index("ep")
     mine = pl.ds(2 * me, 2)
 
-    base_copy = pltpu.make_async_copy(base.at[0], old, base_sem)
-    base_copy.start()
+    base_copies = [
+        pltpu.make_async_copy(base.at[0, :, pl.ds(16 * c, 16)], d.at[pl.ds(32 * c, 32)], base_sem.at[c]) for c in range(7)
+    ]
+    for copy in base_copies:
+        copy.start()
 
     def stored(i, k):
         block, high, wide = tile(i, CHUNKS[k])
@@ -212,15 +215,17 @@
         own2(k).start()
         push(lambda t, k=k: outs[k].at[t], lambda t, k=k: landed(k), s2sem.at[k], r2sem.at[k])
 
-    base_copy.wait()
+    for copy in base_copies:
+        copy.wait()
     g[...] = jnp.zeros_like(g)
 
     def first(c, car):
         rows = pl.ds(pl.multiple_of(c * 16, 16), 16)
-        apart = win[:, rows, :].reshape(C, 1024).astype(F32) - old[:, rows, :].reshape(C, 1024).astype(F32)
-        dc = apart.astype(BF)
+        held = pl.ds(pl.multiple_of(c * 32, 32), 32)
         here = pl.ds(pl.multiple_of(c * C, C), C)
-        d[here, :] = dc
+        dc = (win[:, rows, :].astype(F32) - d[held].astype(F32)).astype(BF)
+        d[held] = dc
+        dc = dc.reshape(C, 1024)
         y = dot(st, dc, NT)
         yt[:, here] = y
         g[...] += gram(y)
@@ -234,6 +239,9 @@
 
     halves = (pl.ds(0, HALF), pl.ds(HALF, HALF))
 
+    def delta(n):
+        return d[112 * n : 112 * (n + 1)].reshape(HALF, 1024)
+
     def step(t, car):
         chol_inv(g, w, spread)
         left = wide_left(w[...])
@@ -241,9 +249,9 @@
         @pl.when(t % 2 == 0)
         def _():
             total = jnp.zeros((K, 1024), F32)
-            for h in halves:
+            for n, h in enumerate(halves):
                 q = dot(left, wide_right(yt[:, h]), NN)
-                total = total + dot(q.astype(BF), d[h, :], NN)
+                total = total + dot(q.astype(BF), delta(n), NN)
             zt[...] = total
             g[...] = gram(total)
 
@@ -251,8 +259,8 @@
         def _():
             across = dot(left, wide_right(zt[...]), NN).astype(BF)
             total = jnp.zeros((K, K), F32)
-            for h in halves:
-                y = dot(across, d[h, :], NT)
+            for n, h in enumerate(halves):
+                y = dot(across, delta(n), NT)
                 yt[:, h] = y
                 total = total + gram(y)
             g[...] = total
@@ -284,8 +292,8 @@
     pl.when(relay)(own_q.start)
 
     total = jnp.zeros((K, 1024), F32)
-    for h in halves:
-        total = total + dot(yt[:, h].astype(BF), d[h, :], NN)
+    for n, h in enumerate(halves):
+        total = total + dot(yt[:, h].astype(BF), delta(n), NN)
     for j in range(8):
         projected[K * j : K * (j + 1), :] = total[:, K * j : K * (j + 1)].astype(BF)
     push(lambda t: projected_rows(projected, t), lambda t: got_p.at[me], psem.at[0], psem.at[1], lambda t: t % 2 == 0)
@@ -359,8 +367,7 @@
         + [pltpu.VMEM((N, rows, 256), BF) for _, rows in CHUNKS]
         + [
             pltpu.VMEM((32, 112, 1024), BF),
-            pltpu.VMEM((32, 112, 1024), BF),
-            pltpu.VMEM((ROWS, 1024), BF),
+            pltpu.VMEM((224, 16, 1024), BF),
             pltpu.VMEM((K, ROWS), F32),
             pltpu.VMEM((K, 1024), F32),
             pltpu.VMEM((K, K), F32),
@@ -374,8 +381,8 @@
             pltpu.VMEM((N, 16, K), BF),
         ]
         + [pltpu.SemaphoreType.DMA((parts,))] * 6
-        + [pltpu.SemaphoreType.DMA, pltpu.SemaphoreType.DMA((6,)), pltpu.SemaphoreType.DMA((6,))],
-        compiler_params=pltpu.CompilerParams(has_side_effects=True, vmem_limit_bytes=58 * 2**20),
+        + [pltpu.SemaphoreType.DMA((7,)), pltpu.SemaphoreType.DMA((6,)), pltpu.SemaphoreType.DMA((6,))],
+        compiler_params=pltpu.CompilerParams(has_side_effects=True, vmem_limit_bytes=47 * 2**20),
         name="relocate_and_factor",
     )(adjusted_of, result_of, adjusted.reshape(2, 32, 112, 1024), base.reshape(1, 32, 112, 1024), sketch)
 

time: 327 us -> 326 us (level)
  no operation moved by 1% of the time
where the time goes in v6:
time: 326 us; the launch traced here: 325 us
  Pallas kernels  320 us (98%)
    pallas_call x1, Pallas kernels, relocate_and_factor(): pl.pallas_call(kernel, out_shape=(jax.ShapeDtypeStruct((32, 112, K), BF),...  320 us

profile of v6, /device:TPU:1, one launch (start us, length us, event | category | flops | bytes accessed | tf_op | source)
XLA Modules:
  0.0 325.4 jit_solution(5245545513319482180)
XLA Ops:
  0.6 0.8 select_reduce_fusion
  1.4 0.0 copy-start
  1.4 0.9 copy-done
  2.4 320.4 %relocate_and_factor.1 = (bf16[32,112,128]{2,1,0:T(8,128)(2,1)S(1)}, bf16[1024,128]{1,0:T(8,128)(2,1)S(1)}) custom-call(s32[128]{0:T(128)S(1)} %get-tuple-element.7.adjusted_of, s32[128]{0:T(128)S(1)} %get-tuple-element.6.result_of, bf16[2,32,112,1024]{3,2,1,0:T(8,128)(2,1)} %bitcast.8, bf16[1,32,112,1024]{3,2,1,0:T(8,128)(2,1)} %bitcast.9, ...), custom_call_target="tpu_custom_call" | custom-call | tf_op jit(solution)/shard_map/relocate_and_factor/pallas_call | solution.py:361
  322.8 1.4 convert_multiply_fusion
  324.2 0.3 copy.9
  324.5 0.9 reshape.37
  (1 shorter events, 0.0 us)
Async XLA Ops:
  1.4 1.0 copy-start

commit v7 on v6

--- a/solution.py
+++ b/solution.py
@@ -170,6 +170,12 @@
     return ref.at[pl.ds(pl.multiple_of((i // 2) * 16, 16), 16)]
 
 
+def projected_tile(ref, i):
+    unit = lax.div(i, 2)
+    high = pl.ds(pl.multiple_of(lax.rem(unit, 8) * 16, 16), 16)
+    return ref.at[high, pl.ds(pl.multiple_of(lax.div(unit, 8) * K, K), K)]
+
+
 def kernel(adjusted_of, result_of, adjusted, base, sketch, basis_out, projected_out, *scratch):
     parts = len(CHUNKS)
     gots = scratch[:parts]
@@ -286,7 +292,7 @@
     own_q = pltpu.make_async_copy(basis.at[lax.rem(place, 112)], got_q.at[me], qsem.at[4])
     own_q2 = pltpu.make_async_copy(out_q.at[me], basis_rows(basis_out, place), qsem.at[5])
     own_p = pltpu.make_async_copy(projected_rows(projected, me), got_p.at[me], psem.at[4])
-    own_p2 = pltpu.make_async_copy(out_p.at[me], projected_rows(projected_out, me), psem.at[5])
+    own_p2 = pltpu.make_async_copy(out_p.at[me], projected_tile(projected_out, me), psem.at[5])
 
     push(lambda t: basis.at[entry(t)], lambda t: got_q.at[me], qsem.at[0], qsem.at[1], lambda t: entry(t) < 112)
     pl.when(relay)(own_q.start)
@@ -323,7 +329,7 @@
 
         lax.fori_loop(0, N, pick, 0, unroll=4)
         own_p2.start()
-        push(lambda t: out_p.at[t], lambda t: projected_rows(projected_out, me), psem.at[2], psem.at[3])
+        push(lambda t: out_p.at[t], lambda t: projected_tile(projected_out, me), psem.at[2], psem.at[3])
 
     for k in range(parts):
         wait_for(gots[k], 2 * (N - 1), ssem.at[k])
@@ -360,7 +366,7 @@
     parts = len(CHUNKS)
     return pl.pallas_call(
         kernel,
-        out_shape=(jax.ShapeDtypeStruct((32, 112, K), BF), jax.ShapeDtypeStruct((1024, K), BF)),
+        out_shape=(jax.ShapeDtypeStruct((32, 112, K), BF), jax.ShapeDtypeStruct((K, 1024), BF)),
         in_specs=[smem, smem, anywhere, anywhere, pl.BlockSpec(memory_space=pltpu.VMEM)],
         out_specs=(anywhere, anywhere),
         scratch_shapes=[pltpu.VMEM((2 * N, rows, 256), BF) for _, rows in CHUNKS]
@@ -397,8 +403,7 @@
     result_of = by_key(owner_map, base_place)
     basis, projected = relocate_and_factor(adjusted_of, result_of, adjusted_tiles, base_tiles, sketch)
     scaled_basis = basis.reshape(ROWS, K).astype(F32) * math.sqrt(ROWS)
-    projected = projected.astype(F32).reshape(8, K, K).transpose(1, 0, 2).reshape(K, 1024)
-    return (scaled_basis[None], projected[None])
+    return (scaled_basis[None], projected.astype(F32)[None])
 
 
 def solution(mesh):

time: 326 us -> 325 us (level)
  no operation moved by 1% of the time
where the time goes in v7:
time: 325 us
  Pallas kernels  320 us (98%)
    pallas_call x1, Pallas kernels, relocate_and_factor(): pl.pallas_call(kernel, out_shape=(jax.ShapeDtypeStruct((32, 112, K), BF),...  320 us

profile of v7, /device:TPU:1, one launch (start us, length us, event | category | flops | bytes accessed | tf_op | source)
XLA Modules:
  0.0 325.0 jit_solution(17154017164777588773)
XLA Ops:
  0.6 0.8 select_reduce_fusion
  1.4 0.0 copy-start
  1.4 0.9 copy-done
  2.4 320.4 %relocate_and_factor.1 = (bf16[32,112,128]{2,1,0:T(8,128)(2,1)S(1)}, bf16[128,1024]{1,0:T(8,128)(2,1)S(1)}) custom-call(s32[128]{0:T(128)S(1)} %get-tuple-element.7.adjusted_of, s32[128]{0:T(128)S(1)} %get-tuple-element.6.result_of, bf16[2,32,112,1024]{3,2,1,0:T(8,128)(2,1)} %bitcast.6, bf16[1,32,112,1024]{3,2,1,0:T(8,128)(2,1)} %bitcast.7, ...), custom_call_target="tpu_custom_call" | custom-call | tf_op jit(solution)/shard_map/relocate_and_factor/pallas_call | solution.py:367
  322.8 1.4 convert_multiply_fusion
  324.1 0.8 bitcast_convert_fusion
Async XLA Ops:
  1.4 1.0 copy-start
